TPU v7x, 256 devices: a whole 4x4x8 slice. The times are simulated.
256 devices in a mesh: tile: 128 (over x, y, z_hi, core), slab: 2 (over z_lo).
Axes of the slice: x: 4, y: 4, z: 8 (z_hi: 4, z_lo: 2; z = z_hi * 2 + z_lo), core: 2. Of those that a mesh axis runs over, the one named last changes fastest.
Arguments:
- volume: bfloat16 [128, 128, 2048], P('tile', 'slab'), may hold values from -6 to 6
- fov_mask: int32 [128, 2048], P('tile'), may hold values from 0 to 1, as said below
- block_angles: int32 [16], replicated, may hold values from 0 to 149
- row_range: int32 [128, 2], replicated, may hold values from 0 to 64, as said below
Outputs:
- sinogram: float32 [128, 64, 1024], P('tile', 'slab')
Inputs may be any that keep to these rules, and one draw needn't show every extreme that they name: fov_mask[t, p] is 1 exactly where the voxel lies inside a region about the volume's centre whose extent along y is set separately for each voxel column x. row_range[v, 0] < row_range[v, 1] for every view.
All inputs are finite; a program needn't handle non-finite values.
Results may differ from a plain program's by a relative error of at most 0.0029.
Values sent between devices are 32-bit elements; how exact they have to be, the bound alone decides.
A program may use at most 64 MiB of HBM per device.

v0:
```python
import math

import jax
import jax.numpy as jnp
from jax import lax
from jax.sharding import PartitionSpec as P

COLS = 1024
WIN = 128
R_SLAB = 32
HALO = 4
TX = 32
TY = 64
GRID_X = 16
CZ = 64


def shifted(block, axis, distance):
    devices = range(lax.axis_size(axis))
    route = [((i - distance) % len(devices), i) for i in devices]
    return lax.ppermute(block, axis, route)


def passed_along(x, axis, by):
    devices = lax.axis_size(axis)
    pairs = [(i, i + by) for i in range(devices) if 0 <= i + by < devices]
    return lax.ppermute(x, axis, pairs)


def view_geometry(block_angles, view_id):
    angle_index = block_angles[view_id // 8] + 150 * (view_id % 8)
    angle_rad = angle_index.astype(jnp.float32) * (2.0 * math.pi / 1200.0)
    cos_part = jnp.cos(angle_rad)
    sin_part = jnp.sin(angle_rad)
    spread = jnp.maximum(jnp.abs(cos_part), jnp.abs(sin_part))
    magnify = 1.3 + 0.35 * cos_part
    return (
        cos_part,
        sin_part,
        magnify,
        magnify * spread,
        1.0 / spread,
        2.5 * sin_part,
        R_SLAB / CZ * magnify / 1.65,
    )


def snake_position(tile_id):
    grid_row = tile_id // GRID_X
    along_row = tile_id % GRID_X
    grid_col = jnp.where(grid_row % 2 == 0, along_row, GRID_X - 1 - along_row)
    return (grid_col, grid_row)


def window_start(grid_col, grid_row, geometry, half_x, half_y):
    cos_part, sin_part, magnify = geometry[:3]
    tile_x = (grid_col * TX).astype(jnp.float32) + TX / 2 - half_x
    tile_y = (grid_row * TY).astype(jnp.float32) + TY / 2 - half_y
    tile_centre = COLS / 2 + magnify * (tile_x * cos_part + tile_y * sin_part)
    return jnp.clip(jnp.floor(tile_centre).astype(jnp.int32) - WIN // 2, 0, COLS - WIN)


def transaxial(grid_col, grid_row, geometry, half_x, half_y):
    cos_part, sin_part, magnify, box_width, amplitude = geometry[:5]
    pixels = jnp.arange(TX * TY, dtype=jnp.int32)
    x_pos = (grid_col * TX + pixels // TY).astype(jnp.float32) + 0.5 - half_x
    y_pos = (grid_row * TY + pixels % TY).astype(jnp.float32) + 0.5 - half_y
    centre = COLS / 2 + magnify * (x_pos * cos_part + y_pos * sin_part)
    first_col = window_start(grid_col, grid_row, geometry, half_x, half_y)
    col_edges = (first_col + jnp.arange(WIN, dtype=jnp.int32)).astype(jnp.float32)
    low_end = jnp.maximum(centre[:, None] - box_width / 2, col_edges[None, :])
    high_end = jnp.minimum(centre[:, None] + box_width / 2, col_edges[None, :] + 1.0)
    footprint = (jnp.maximum(high_end - low_end, 0.0) * amplitude).astype(jnp.bfloat16)
    return (footprint, first_col)


def axial_footprint(row_index, z_pos, geometry, total_rows):
    row_shift, axial_width = (geometry[5], geometry[6])
    centre = total_rows / 2 + row_shift + axial_width * z_pos
    row_float = row_index.astype(jnp.float32)
    low_end = jnp.maximum(centre[None, :] - axial_width / 2, row_float[:, None])
    high_end = jnp.minimum(centre[None, :] + axial_width / 2, row_float[:, None] + 1.0)
    return jnp.maximum(high_end - low_end, 0.0)


def on_device(volume, fov_mask, block_angles, row_range):
    tile_count = lax.axis_size("tile")
    slab_count = lax.axis_size("slab")
    tile_id = lax.axis_index("tile")
    slab_id = lax.axis_index("slab")
    grid_col, grid_row = snake_position(tile_id)
    half_x = GRID_X * TX / 2
    half_y = tile_count // GRID_X * TY / 2
    depth_z = volume.shape[1]
    masked = volume[0] * fov_mask[0][None, :].astype(jnp.bfloat16)
    band_rows = R_SLAB + 2 * HALO
    row_index = slab_id * R_SLAB - HALO + jnp.arange(band_rows, dtype=jnp.int32)
    z_pos = (
        (slab_id * depth_z + jnp.arange(depth_z, dtype=jnp.int32)).astype(jnp.float32)
        + 0.5
        - depth_z * slab_count / 2
    )

    def contribution(view_id):
        geometry = view_geometry(block_angles, view_id)
        footprint, first_col = transaxial(grid_col, grid_row, geometry, half_x, half_y)
        partial_value = jnp.dot(masked, footprint, preferred_element_type=jnp.float32)
        weights = axial_footprint(row_index, z_pos, geometry, R_SLAB * slab_count)
        band_sum = jnp.dot(
            weights,
            partial_value,
            precision=lax.Precision.HIGHEST,
            preferred_element_type=jnp.float32,
        )
        return (band_sum, first_col)

    def add_into(running, band_sum, first_col):
        current = lax.dynamic_slice(running, (jnp.int32(0), first_col), (band_rows, WIN))
        return lax.dynamic_update_slice(running, current + band_sum, (jnp.int32(0), first_col))

    blank_rows = jnp.zeros((band_rows, COLS), jnp.float32)

    def cycle_step(turn_id, running):
        view_id = (tile_id + tile_count - 1 - turn_id) % tile_count
        band_sum, first_col = contribution(view_id)
        running = add_into(running, band_sum, first_col)
        return shifted(running, "tile", 1)

    running = lax.fori_loop(0, tile_count - 1, cycle_step, blank_rows)
    band_sum, first_col = contribution(tile_id)
    running = add_into(running, band_sum, first_col)
    from_below = passed_along(running[R_SLAB + HALO :], "slab", 1)
    from_above = passed_along(running[:HALO], "slab", -1)
    own_rows = running[HALO : HALO + R_SLAB]
    own_rows = own_rows.at[:HALO].add(from_below)
    own_rows = own_rows.at[R_SLAB - HALO :].add(from_above)
    global_rows = slab_id * R_SLAB + jnp.arange(R_SLAB, dtype=jnp.int32)
    in_range = (global_rows >= row_range[tile_id, 0]) & (global_rows < row_range[tile_id, 1])
    return jnp.where(in_range[:, None], own_rows, jnp.float32(0.0))[None]


def solution(mesh):
    in_specs = (P("tile", "slab", None), P("tile", None), P(), P())
    out_specs = P("tile", "slab", None)
    return jax.shard_map(
        on_device, mesh=mesh, in_specs=in_specs, out_specs=out_specs, check_vma=False
    )
```

profile of v0, /device:TPU:1, one launch (start us, length us, event | category | flops | bytes accessed | tf_op | source)
XLA Modules:
  0.0 2011.3 jit_solution(4569038109823072681)
XLA Ops:
  4.7 1996.0 %while.21 = (s32[]{:T(128)}, f32[40,1024]{1,0:T(8,128)S(1)}, s32[]{:T(128)}, s32[16]{0:T(128)S(1)}, f32[]{:T(128)}, /*index=5*/f32[]{:T(128)}, s32[]{:T(128)}, s...) while((s32[]{:T(128)}, f32[40,1024]{1,0:T(8,128)S(1)}, ...), condition=%wide.region_1.2_spmd.clone, body=%wide.region_0.1_spmd.clone.sunk | while | flops 39127360 | bytes 1430175 | solution.py:129
  60.5 12.6 collective-permute-done
  139.7 12.6 collective-permute-done
  202.7 12.7 collective-permute-done
  249.9 12.7 collective-permute-done
  281.7 12.6 collective-permute-done
  439.4 12.7 collective-permute-done
  486.6 12.8 collective-permute-done
  550.2 12.6 collective-permute-done
  613.2 12.7 collective-permute-done
  660.8 12.6 collective-permute-done
  755.4 12.7 collective-permute-done
  882.2 12.7 collective-permute-done
  1024.4 12.6 collective-permute-done
  1119.2 12.8 collective-permute-done
  1198.2 12.6 collective-permute-done
  1261.2 12.7 collective-permute-done
  1371.9 12.6 collective-permute-done
  1466.9 12.6 collective-permute-done
  1514.1 12.6 collective-permute-done
  1766.8 12.8 collective-permute-done
  1798.6 12.6 collective-permute-done
  1814.5 12.6 collective-permute-done
  1893.2 12.7 collective-permute-done
  (1658 shorter events, 1604.1 us)
Async XLA Ops:
  60.4 12.7 collective-permute-start
  139.6 12.7 collective-permute-start
  202.6 12.8 collective-permute-start
  249.9 12.8 collective-permute-start
  281.6 12.7 collective-permute-start
  439.3 12.8 collective-permute-start
  455.3 12.7 collective-permute-start
  486.5 12.9 collective-permute-start
  550.1 12.7 collective-permute-start
  613.2 12.8 collective-permute-start
  660.7 12.7 collective-permute-start
  755.3 12.8 collective-permute-start
  882.1 12.8 collective-permute-start
  1024.4 12.7 collective-permute-start
  1119.1 12.9 collective-permute-start
  1198.1 12.7 collective-permute-start
  1261.1 12.8 collective-permute-start
  1371.8 12.7 collective-permute-start
  1466.8 12.7 collective-permute-start
  1514.0 12.7 collective-permute-start
  1766.7 12.9 collective-permute-start
  1798.5 12.7 collective-permute-start
  1814.4 12.7 collective-permute-start
  1893.1 12.8 collective-permute-start
  (108 other events, 1297.5 us)
where the time goes:
time: 2020 us; the launch traced here: 2010 us
  waiting for transfers between devices  1570 us (78%)
  matrix products  152 us (8%)
  local copies, waits for them, and re-layouts  140 us (7%)
  loops' own time  115 us (6%)
  starting transfers between devices  24.4 us (1%)
    ppermute x127, waiting for transfers between devices, shifted(): return lax.ppermute(block, axis, route)  1570 us
    another operation x1, loops' own time, on_device(): running = lax.fori_loop(0, tile_count - 1, cycle_step, blank_rows)  115 us
    dot_general x128, matrix products, contribution(): jnp.dot(masked, footprint, preferred_element_type=jnp.float32)  115 us
    dynamic_slice x128, local copies, waits for them, and re-layouts, view_geometry(): angle_index = block_angles[view_id // 8] + 150 * (view_id % 8)  71.3 us
    dynamic_update_slice x128, local copies, waits for them, and re-layouts, add_into(): lax.dynamic_update_slice(running, current + band_sum, (jnp.int32(0), firs...  64.8 us
  transfers between devices with their start and end apart: 129, of which 128 were waited for; matrix products, arithmetic and copies ran while one was open for 0% of the time, Pallas kernels for 0%

commit v1 on v0

v1 whole, which is shorter than its diff:
```python
import math

import jax
import jax.numpy as jnp
from jax import lax
from jax.experimental import pallas as pl
from jax.experimental.pallas import tpu as pltpu
from jax.sharding import PartitionSpec as P

COLS = 1024
R_SLAB = 32
TX = 32
TY = 64
GRID_X = 16
CZ = 64
SUB = 16
NX = 4
NY = 4
NZH = 4
BLOCKS = NX * NY
SUBS = 16
HALO_Z = 8
F32 = jnp.float32
BF16 = jnp.bfloat16
MESH = pl.DeviceIdType.MESH
WIN_ROWS = (40, 32, 32, 40)
MSG_ROWS = (40, 32, 32, 40)
PAD = 64


def view_geometry(block_angles, view_id):
    angle_index = block_angles[view_id // 8] + 150 * (view_id % 8)
    angle_rad = angle_index.astype(F32) * (2.0 * math.pi / 1200.0)
    cos_part = jnp.cos(angle_rad)
    sin_part = jnp.sin(angle_rad)
    spread = jnp.maximum(jnp.abs(cos_part), jnp.abs(sin_part))
    magnify = 1.3 + 0.35 * cos_part
    return (
        cos_part,
        sin_part,
        magnify,
        magnify * spread,
        1.0 / spread,
        2.5 * sin_part,
        R_SLAB / CZ * magnify / 1.65,
    )


def snake_position(tile_id):
    grid_row = tile_id // GRID_X
    along_row = tile_id % GRID_X
    grid_col = jnp.where(grid_row % 2 == 0, along_row, GRID_X - 1 - along_row)
    return (grid_col, grid_row)


def tables(block_angles, tile_id):
    core = tile_id % 2
    chip = tile_id // 2
    zh = chip % NZH
    block = chip // NZH
    half_x = GRID_X * TX / 2
    half_y = 128 // GRID_X * TY / 2

    views = jnp.arange(128, dtype=jnp.int32)
    c, s, m, b, g, h, e = view_geometry(block_angles, views)
    chips = jnp.arange(64, dtype=jnp.int32)
    col0, row0 = snake_position(2 * chips)
    col1, _ = snake_position(2 * chips + 1)
    sx = (jnp.minimum(col0, col1) * TX).astype(F32) + 0.5 - half_x
    sy = (row0 * TY).astype(F32) + 0.5 - half_y
    corner = COLS / 2 + m[:, None] * (sx[None] * c[:, None] + sy[None] * s[:, None])
    reach = 63.0 * m * (jnp.minimum(c, 0.0) + jnp.minimum(s, 0.0)) - b / 2
    lowest = corner + reach[:, None]
    first4 = jnp.floor((lowest - 0.25) * 0.25).astype(jnp.int32)
    first4 = lax.optimization_barrier(first4)

    order = (jnp.arange(NZH, dtype=jnp.int32)[:, None] * 2 + core
             + 8 * jnp.arange(BLOCKS, dtype=jnp.int32)[None, :]).reshape(-1)
    vc, vs, vm, vb, vg, vh, ve = view_geometry(block_angles, order)
    fpar = jnp.stack(
        [vg * vm * vc, vg * vm * vs, vg, vg * jnp.minimum(vb, 1.0),
         vg * (vb + 1.0) * 0.5, vh, ve, ve],
        axis=1,
    ).reshape(-1)
    sub = jnp.arange(SUBS, dtype=jnp.int32)
    tile_of = jnp.where(sub // 8 == 0, tile_id, 2 * chip + 1 - core)
    gcol, grow = snake_position(tile_of)
    px = (gcol * TX + (sub // 4) % 2 * SUB).astype(F32) + 0.5 - half_x
    py = (grow * TY + sub % 4 * SUB).astype(F32) + 0.5 - half_y
    base = COLS / 2 + vm[:, None] * (px[None] * vc[:, None] + py[None] * vs[:, None])
    low = base + ((SUB - 1.0) * vm * (jnp.minimum(vc, 0.0) + jnp.minimum(vs, 0.0)) - vb / 2)[:, None]
    start = jnp.floor(low)
    fsub = (vg[:, None] * (base - start - 0.5)).reshape(-1)
    own_first = lax.dynamic_index_in_dim(first4, chip, 1, keepdims=False)
    own_first = own_first.reshape(BLOCKS, 8)
    own_first = lax.dynamic_slice(
        jnp.pad(own_first, ((0, 0), (0, 1))), (jnp.int32(0), core), (BLOCKS, 8))[:, ::2]
    own_first = own_first.T.reshape(-1)
    isub = (start.astype(jnp.int32) - 4 * own_first[:, None]).reshape(-1)
    mine = lax.dynamic_slice(
        jnp.pad(first4, ((0, 1), (0, 0))), (block * 8 + core, jnp.int32(0)), (8, 64))[::2]
    roff = lax.dynamic_index_in_dim(
        mine.reshape(NZH, BLOCKS, NZH), zh, 2, keepdims=False).reshape(-1)
    return fpar, fsub, isub, roff


def kernel(fpar, fsub, isub, roff, vol_ref, mask_ref, out_ref,
           own_v, pair_v, own_h, pair_h, wts, res40, res32, axial_rows,
           send0, send1, send2, send3, recv0, recv1, recv2, recv3, summed, arrived,
           vol_send, vol_recv, msg_send, msg_recv, sum_send, sum_recv):
    tile = lax.axis_index("tile")
    slab = lax.axis_index("slab")
    core = lax.rem(tile, 2)
    chip = lax.div(tile, 2)
    zh = lax.rem(chip, NZH)
    block = lax.div(chip, NZH)
    x = lax.div(block, NY)
    y = lax.rem(block, NY)
    sends = (send0, send1, send2, send3)
    recvs = (recv0, recv1, recv2, recv3)

    def device(bx, z, k):
        return (bx * NZH + z) * 2 + k

    partner = 2 * chip + 1 - core
    greeted = [(partner, slab), (tile, 1 - slab), (partner, 1 - slab)]
    for dx in range(NX):
        for dy in range(NY):
            if dx or dy:
                there = lax.rem(x + dx, NX) * NY + lax.rem(y + dy, NY)
                greeted.append((device(there, zh, core), slab))
    for dz in range(1, NZH):
        greeted.append((device(block, lax.rem(zh + dz, NZH), core), slab))
    barrier = pltpu.get_barrier_semaphore()
    for where_to in greeted:
        pl.semaphore_signal(barrier, inc=1, device_id=where_to, device_id_type=MESH)

    own_v[...] = vol_ref[...].astype(F32) * mask_ref[...].astype(F32)
    for res, win in ((res40, 40), (res32, 32)):
        pad = 2 * win

        def clear(j, carry, res=res, win=win, pad=pad):
            res[j, 0:pad, :] = jnp.zeros((pad, 128), F32)
            res[j, pad + win:, :] = jnp.zeros((pad, 128), F32)
            return carry

        lax.fori_loop(0, NY * SUBS, clear, 0)
    for zz in range(NZH):

        def clear(j, carry, zz=zz):
            recvs[zz][j, 0:PAD, :] = jnp.zeros((PAD, 128), F32)
            recvs[zz][j, PAD + MSG_ROWS[zz]:, :] = jnp.zeros((PAD, 128), F32)
            return carry

        lax.fori_loop(0, BLOCKS, clear, 0)

    pl.semaphore_wait(barrier, len(greeted))

    edge = pl.ds(pl.multiple_of((1 - slab) * (CZ - HALO_Z), HALO_Z), HALO_Z)
    give_pair = pltpu.make_async_remote_copy(
        own_v, pair_v, vol_send.at[0], vol_recv.at[0],
        device_id=(partner, slab), device_id_type=MESH)
    give_edge = pltpu.make_async_remote_copy(
        own_v.at[edge], own_h, vol_send.at[1], vol_recv.at[1],
        device_id=(tile, 1 - slab), device_id_type=MESH)
    give_cross = pltpu.make_async_remote_copy(
        own_v.at[edge], pair_h, vol_send.at[2], vol_recv.at[2],
        device_id=(partner, 1 - slab), device_id_type=MESH)
    give_edge.start()
    give_cross.start()
    give_pair.start()

    def take_tile(k, big, halo):
        for pb in range(16):
            cols = slice(pb * 128, (pb + 1) * 128)
            part = jnp.concatenate(
                [big[:, cols], halo[:, cols], jnp.zeros((128 - CZ - HALO_Z, 128), F32)], axis=0)
            turned = part.T.astype(BF16)
            for x2 in range(2):
                xb, xi = divmod(pb * 2 + x2, SUB)
                for yb in range(4):
                    rows = slice(x2 * 64 + yb * SUB, x2 * 64 + yb * SUB + SUB)
                    wts[k * 8 + xb * 4 + yb, xi * SUB:(xi + 1) * SUB, :] = turned[rows]

    give_edge.wait()
    take_tile(0, own_v, own_h)
    give_cross.wait()
    give_pair.wait()
    take_tile(1, pair_v, pair_h)

    pix = lax.broadcasted_iota(jnp.int32, (8, SUB * SUB), 1)
    pix_x = lax.div(pix, SUB).astype(F32)
    pix_y = lax.rem(pix, SUB).astype(F32)
    lane = lax.broadcasted_iota(jnp.int32, (80, 128), 1)
    zrow = lax.broadcasted_iota(jnp.int32, (80, 128), 0)
    row_low = (lax.rem(lane, R_SLAB) + slab * R_SLAB).astype(F32)
    slice_id = jnp.where(
        zrow < CZ, zrow + slab * CZ,
        jnp.where(slab == 0, zrow, zrow - HALO_Z)).astype(F32)
    z_pos = slice_id + (0.5 - CZ)

    def project(zz, dx):
        win, msg = WIN_ROWS[zz], MSG_ROWS[zz]
        res = res40 if win == 40 else res32
        pad = 2 * win
        half = 2 * msg
        krow = lax.broadcasted_iota(jnp.int32, (win, SUB * SUB), 0).astype(F32)
        bx = lax.rem(x + dx, NX)
        ids = [zz * BLOCKS + bx * NY + lax.rem(y + dy, NY) for dy in range(NY)]
        pre = []
        for v in ids:
            line = fpar[v * 8] * pix_x + fpar[v * 8 + 1] * pix_y
            pre.append(
                jnp.concatenate([line] * (win // 8), axis=0) - fpar[v * 8 + 2] * krow)
        for i in range(SUBS):
            parts = []
            for dy, v in enumerate(ids):
                dist = jnp.abs(pre[dy] + fsub[v * SUBS + i])
                parts.append(jnp.minimum(fpar[v * 8 + 4] - dist, fpar[v * 8 + 3]))
            foot = jnp.maximum(jnp.concatenate(parts, axis=0).astype(BF16), jnp.zeros((), BF16))
            got = jnp.dot(foot, wts[i], preferred_element_type=F32)
            for dy in range(NY):
                res[dy * SUBS + i, pad:pad + win, :] = got[dy * win:(dy + 1) * win]
        for dy, v in enumerate(ids):
            chunks = []
            for ch in range(2):
                total = None
                for i in range(SUBS):
                    at = pad + ch * half - isub[v * SUBS + i]
                    at = jnp.minimum(jnp.maximum(at, 0), pad + win)
                    term = res[dy * SUBS + i, pl.ds(at, half), :]
                    total = term if total is None else total + term
                chunks.append(total)
            part = jnp.concatenate(chunks, axis=0)
            high = part.astype(BF16)
            low = (part - high.astype(F32)).astype(BF16)
            h, e = fpar[v * 8 + 5], fpar[v * 8 + 6]
            centre = (R_SLAB + h) + e * z_pos
            axial = jnp.maximum(
                jnp.minimum(centre + e * 0.5, row_low + 1.0)
                - jnp.maximum(centre - e * 0.5, row_low), 0.0)
            a_high = axial.astype(BF16)
            a_low = (axial - a_high.astype(F32)).astype(BF16)
            blank = jnp.zeros((48, 128), BF16)
            a_high = jnp.concatenate([a_high, blank], axis=0)
            a_low = jnp.concatenate([a_low, blank], axis=0)
            axial_rows[dy, 0:4 * msg, :] = (
                jnp.dot(jnp.concatenate([high, low], axis=1),
                        jnp.concatenate([a_high, a_high], axis=0), preferred_element_type=F32)
                + jnp.dot(high, a_low, preferred_element_type=F32))
            quarter = lax.broadcasted_iota(jnp.int32, (msg, 128), 1)
            packed = axial_rows[dy, pl.ds(3, msg, stride=4), :]
            for q in (2, 1, 0):
                packed = jnp.where(quarter < 32 * (q + 1), axial_rows[dy, pl.ds(q, msg, stride=4), :], packed)
            sends[zz][dx * NY + dy] = packed
            away = message(zz, dx, dy)
            if dy == 0:
                @pl.when(dx == 0)
                def _():
                    keep(zz).start()

                @pl.when(dx != 0)
                def _():
                    away.start()
            else:
                away.start()

    def message(zz, dx, dy):
        there = lax.rem(x + dx, NX) * NY + lax.rem(y + dy, NY)
        return pltpu.make_async_remote_copy(
            sends[zz].at[dx * NY + dy],
            recvs[zz].at[block, pl.ds(PAD, MSG_ROWS[zz])],
            msg_send.at[zz, dx * NY + dy], msg_recv.at[zz, block],
            device_id=(device(there, zh, core), slab), device_id_type=MESH)

    def keep(zz):
        return pltpu.make_async_copy(
            sends[zz].at[0], recvs[zz].at[block, pl.ds(PAD, MSG_ROWS[zz])],
            msg_recv.at[zz, block])

    def arrival(zz, src):
        return pltpu.make_async_remote_copy(
            sends[zz].at[0], recvs[zz].at[src, pl.ds(PAD, MSG_ROWS[zz])],
            msg_send.at[zz, 0], msg_recv.at[zz, src],
            device_id=(device(src, zh, core), slab), device_id_type=MESH)

    def total_out(zz):
        return pltpu.make_async_remote_copy(
            summed.at[zz], arrived.at[zh], sum_send.at[zz], sum_recv.at[zh],
            device_id=(device(block, zz, core), slab), device_id_type=MESH)

    def total_keep(zz):
        return pltpu.make_async_copy(summed.at[zz], arrived.at[zh], sum_recv.at[zh])

    def gather_block(zz):
        msg = MSG_ROWS[zz]

        def await_one(src, carry):
            @pl.when(src == block)
            def _():
                keep(zz).wait()

            @pl.when(src != block)
            def _():
                arrival(zz, src).wait_recv()
            return carry

        lax.fori_loop(0, BLOCKS, await_one, 0)
        for ch in range(4):
            total = None
            for src in range(BLOCKS):
                at = PAD + PAD * ch - roff[zz * BLOCKS + src]
                at = jnp.minimum(jnp.maximum(at, 0), PAD + msg)
                term = recvs[zz][src, pl.ds(at, PAD), :]
                total = term if total is None else total + term
            summed[zz, ch * PAD:(ch + 1) * PAD, :] = total

        @pl.when(zh == zz)
        def _():
            total_keep(zz).start()

        @pl.when(zh != zz)
        def _():
            total_out(zz).start()

    for zz in range(NZH):
        def step(dx, carry, zz=zz):
            project(zz, dx)
            return carry

        lax.fori_loop(0, NX, step, 0)
        if zz:
            gather_block(zz - 1)
    gather_block(NZH - 1)

    def await_total(src, carry):
        @pl.when(src == zh)
        def _():
            total_keep(src).wait()

        @pl.when(src != zh)
        def _():
            pltpu.make_async_remote_copy(
                summed.at[0], arrived.at[src], sum_send.at[0], sum_recv.at[src],
                device_id=(device(block, src, core), slab), device_id_type=MESH).wait_recv()
            total_out(src).wait_send()
        return carry

    lax.fori_loop(0, NZH, await_total, 0)
    out_ref[...] = (arrived[0] + arrived[1]) + (arrived[2] + arrived[3])
    for zz in range(NZH):
        def drain(n, carry, zz=zz):
            message(zz, lax.div(n, NY), lax.rem(n, NY)).wait_send()
            return carry

        lax.fori_loop(1, BLOCKS, drain, 0)


def on_device(volume, fov_mask, block_angles, row_range):
    tile_id = lax.axis_index("tile")
    slab_id = lax.axis_index("slab")
    fpar, fsub, isub, roff = tables(block_angles, tile_id)
    smem = pl.BlockSpec(memory_space=pltpu.SMEM)
    vmem = pl.BlockSpec(memory_space=pltpu.VMEM)
    packed = pl.pallas_call(
        kernel,
        out_shape=jax.ShapeDtypeStruct((COLS // 4, 128), F32),
        in_specs=[smem] * 4 + [vmem] * 2,
        out_specs=vmem,
        scratch_shapes=[
            pltpu.VMEM((CZ, TX * TY), F32),
            pltpu.VMEM((CZ, TX * TY), F32),
            pltpu.VMEM((HALO_Z, TX * TY), F32),
            pltpu.VMEM((HALO_Z, TX * TY), F32),
            pltpu.VMEM((SUBS, SUB * SUB, 128), BF16),
            pltpu.VMEM((NY * SUBS, 200, 128), F32),
            pltpu.VMEM((NY * SUBS, 160, 128), F32),
            pltpu.VMEM((NY, 160, 128), F32),
            *[pltpu.VMEM((BLOCKS, r, 128), F32) for r in MSG_ROWS],
            *[pltpu.VMEM((BLOCKS, r + 2 * PAD, 128), F32) for r in MSG_ROWS],
            pltpu.VMEM((NZH, COLS // 4, 128), F32),
            pltpu.VMEM((NZH, COLS // 4, 128), F32),
            pltpu.SemaphoreType.DMA((3,)),
            pltpu.SemaphoreType.DMA((3,)),
            pltpu.SemaphoreType.DMA((NZH, BLOCKS)),
            pltpu.SemaphoreType.DMA((NZH, BLOCKS)),
            pltpu.SemaphoreType.DMA((NZH,)),
            pltpu.SemaphoreType.DMA((NZH,)),
        ],
        compiler_params=pltpu.CompilerParams(
            collective_id=0, has_side_effects=True, vmem_limit_bytes=52 * 1024 * 1024),
        cost_estimate=pl.CostEstimate(
            flops=64 * 16 * 40 * 256 * 128 * 2, bytes_accessed=1 << 20, transcendentals=0),
    )(fpar, fsub, isub, roff, volume[0], fov_mask)
    rows = packed.reshape(COLS // 4, 4, R_SLAB).transpose(2, 0, 1).reshape(R_SLAB, COLS)
    global_rows = slab_id * R_SLAB + jnp.arange(R_SLAB, dtype=jnp.int32)
    in_range = (global_rows >= row_range[tile_id, 0]) & (global_rows < row_range[tile_id, 1])
    return jnp.where(in_range[:, None], rows, F32(0.0))[None]


def solution(mesh):
    in_specs = (P("tile", "slab", None), P("tile", None), P(), P())
    out_specs = P("tile", "slab", None)
    return jax.shard_map(
        on_device, mesh=mesh, in_specs=in_specs, out_specs=out_specs, check_vma=False
    )
```

time: 2020 us -> 74.6 us (0.04)
  waiting for transfers between devices: 1570 us -> 0 us
  matrix products: 152 us -> 0 us
  local copies, waits for them, and re-layouts: 140 us -> 7.14 us
  loops' own time: 115 us -> 0 us
  Pallas kernels: 0 us -> 54.8 us
  starting transfers between devices: 24.4 us -> 0 us
    ppermute x129 -> x0, waiting for transfers between devices: 1570 us -> none  [the longest x127 1570 us: shifted(): return lax.ppermute(block, axis, route)]
    dot_general x256 -> x0, matrix products: 152 us -> none  [the longest x128 115 us: contribution(): jnp.dot(masked, footprint, preferred_element_type=jnp.float32)]
    another operation x1 -> x0, loops' own time: 115 us -> none  [on_device(): running = lax.fori_loop(0, tile_count - 1, cycle_step, blank_rows)]
    dynamic_slice x128 -> x4, local copies, waits for them, and re-layouts: 71.3 us -> 0.2 us  [the longest x1 0.08 us: tables(): lax.dynamic_slice(jnp.pad(own_first, ((0, 0), (0, 1))), (jnp.int32(0), co...]
    dynamic_update_slice x128 -> x0, local copies, waits for them, and re-layouts: 64.8 us -> none  [add_into(): lax.dynamic_update_slice(running, current + band_sum, (jnp.int32(0), firs...]
    pallas_call x0 -> x1, Pallas kernels: none -> 54.8 us  [on_device(): pl.pallas_call(kernel, out_shape=jax.ShapeDtypeStruct((COLS // 4, 128), F...]
    ppermute x129 -> x0, starting transfers between devices: 24.4 us -> none  [the longest x127 18.4 us: shifted(): return lax.ppermute(block, axis, route)]
  transfers between devices with their start and end apart: 129 -> 0, of which waited for: 128 -> 0; matrix products, arithmetic and copies ran while one was open for 0% -> 0% of each run, Pallas kernels for 0% -> 0%
where the time goes in v1:
time: 74.6 us; the launch traced here: 74 us
  Pallas kernels  54.8 us (73%)
  other arithmetic  11.8 us (16%)
  local copies, waits for them, and re-layouts  7.14 us (10%)
    pallas_call x1, Pallas kernels, on_device(): pl.pallas_call(kernel, out_shape=jax.ShapeDtypeStruct((COLS // 4, 128), F...  54.8 us
    cos x2, other arithmetic, view_geometry(): cos_part = jnp.cos(angle_rad)  10.1 us
    unnamed x9, local copies, waits for them, and re-layouts  2.06 us

profile of v1, /device:TPU:1, one launch (start us, length us, event | category | flops | bytes accessed | tf_op | source)
XLA Modules:
  0.0 74.0 jit_solution(18282220288214325936)
XLA Ops:
  0.1 0.7 copy-done.3
  0.7 0.6 constant_dynamic-slice_fusion.2
  1.3 1.3 %compare_and_fusion = pred[32]{0:T(512)(128)(4,1)S(1)} fusion(s32[]{:T(128)} %bitcast.1, s32[]{:T(128)} %bitcast, s32[]{:T(128)S(6)} %mul.530), kind=kLoop, calls=%fused_computation.60 | loop fusion | flops 128 | bytes 44 | tf_op jit(solution)/shard_map/and | solution.py:397
  2.7 0.1 add.596
  2.8 0.1 add.604
  2.9 0.6 copy-done.2
  3.6 0.8 %gather_fusion = s32[64]{0:T(128)S(1)} fusion(s32[16]{0:T(128)S(1)} %copy-done.2, s32[1024]{0:T(1024)S(1)} %pad_clamp_fusion), kind=kCustom, calls=%fused_computation | custom fusion | bytes 768 | tf_op jit(solution)/shard_map/gather | solution.py:32
  4.7 0.7 fusion.29
  5.4 10.0 %fusion.25 = (f32[128]{0:T(128)S(1)}, f32[128]{0:T(128)S(1)}) fusion(s32[]{:T(128)} %bitcast.28, s32[]{:T(128)} %bitcast.27, s32[]{:T(128)} %bitcast.26, s32[]{:T(128)} %bitcast.25, s32[]{:T(128)} %bitcast.24, s32[]{:T(128)} %bitcast.23, s32[]{:T(128)} %bitcast.22, s32[]{:T(128)} %bitcast.21, s32[]{:T(128)} %bitcast.19, s32[]{:T(128)} %bitcast.17, ...), kind=kLoop, calls=%fused_computation.133 | loop fusion | flops 6528 | bytes 1088 | tf_op jit(solution)/shard_map/cos | solution.py:34
  15.5 0.1 copy.18
  15.6 0.1 copy.17
  15.7 0.1 reshape.661.fpar
  15.8 0.1 floor_convert_fusion
  16.0 0.1 slice.7
  16.2 0.1 reshape.664.roff
  16.6 0.1 copy.19
  16.7 0.1 mul.600
  16.8 0.1 sub.139
  17.0 0.1 add.622
  17.3 0.7 copy-done.1
  17.9 54.8 %shard_map.46 = f32[256,128]{1,0:T(8,128)S(1)} custom-call(f32[512]{0:T(512)S(1)} %reshape.661.fpar, f32[1024]{0:T(1024)S(1)} %add_multiply_fusion.fsub, s32[1024]{0:T(1024)S(1)} %convert_subtract_fusion.isub, s32[64]{0:T(128)S(1)} %reshape.664.roff, bf16[64,2048]{1,0:T(8,128)(2,1)S(1)} %bitcast.142, s32[1,2048]{1,0:T(1,128)S(1)} %copy-done.1), custom_call_target="tpu_custom_call" | custom-call | flops 2684354560 | bytes 1048576 | tf_op jit(solution)/shard_map/pallas_call | solution.py:365
  72.8 0.1 copy.21
  72.9 0.2 copy.22
  73.2 0.8 %copy.23 = f32[1,32,1024]{2,1,0:T(8,128)} copy(f32[1,32,1024]{1,2,0:T(8,128)S(1)} %broadcast_select_fusion) | data formatting | bytes 262144 | tf_op jit(solution)/shard_map/jit(_where)/select_n | solution.py:398
  (39 shorter events, 1.4 us)
Async XLA Ops:
  0.0 0.7 copy-start.3
  2.9 0.7 copy-start.2
  15.8 1.4 %copy-start = (bf16[1,64,2048]{2,1,0:T(8,128)(2,1)S(1)}, bf16[1,64,2048]{2,1,0:T(8,128)(2,1)}, u32[]{:S(2)}) copy-start(bf16[1,64,2048]{2,1,0:T(8,128)(2,1)} %param.4) | copy-start | bytes 786436
  17.2 0.7 copy-start.1

commit v2 on v1

v2 whole, which is shorter than its diff:
```python
import math

import jax
import jax.numpy as jnp
from jax import lax
from jax.experimental import pallas as pl
from jax.experimental.pallas import tpu as pltpu
from jax.sharding import PartitionSpec as P

COLS = 1024
R_SLAB = 32
TX = 32
TY = 64
GRID_X = 16
CZ = 64
SUB = 16
NX = 4
NY = 4
NZH = 4
BLOCKS = NX * NY
SUBS = 16
HALO_Z = 8
F32 = jnp.float32
BF16 = jnp.bfloat16
MESH = pl.DeviceIdType.MESH
WIN_ROWS = (40, 32, 32, 40)
MSG_ROWS = (40, 32, 32, 40)
SENT_ROWS = (37, 26, 26, 37)
PAD = 64
RECV_ROWS = tuple(r + 2 * PAD for r in MSG_ROWS)


def fill_tables(angles, tile, zh, block, core, real, whole):
    shape = (72, 128)
    row = lax.broadcasted_iota(jnp.int32, shape, 0)
    lane = lax.broadcasted_iota(jnp.int32, shape, 1)
    own = row < 64
    zz = jnp.where(own, row >> 4, row & 3)
    angle = jnp.zeros(shape, jnp.int32) + angles[block]
    for k in range(BLOCKS):
        angle = jnp.where(own & ((row & 15) == k), angles[k], angle)
    angle = angle + 150 * (2 * zz + core)
    theta = angle.astype(F32) * (2.0 * math.pi / 1200.0)
    c, s = jnp.cos(theta), jnp.sin(theta)
    spread = jnp.maximum(jnp.abs(c), jnp.abs(s))
    m = 1.3 + 0.35 * c
    b = m * spread
    g = 1.0 / spread
    sub = lane < SUBS
    chip2 = jnp.where(own, tile - core, ((lane - SUBS) * NZH + zh) * 2)
    tiles = jnp.where(sub, jnp.where(lane < 8, tile, tile + 1 - 2 * core), chip2)
    along = tiles & 15
    grow = tiles >> 4
    back = jnp.where(sub, 15, 14) - along
    gcol = jnp.where((grow & 1) == 1, back, along)
    off_x = jnp.where(sub, ((lane >> 2) & 1) * SUB, 0)
    off_y = jnp.where(sub, (lane & 3) * SUB, 0)
    px = (gcol * TX + off_x).astype(F32) + (0.5 - GRID_X * TX / 2)
    py = (grow * TY + off_y).astype(F32) + (0.5 - 128 // GRID_X * TY / 2)
    base = COLS / 2 + m * (px * c + py * s)
    extent = jnp.where(sub, SUB - 1.0, 4.0 * SUB - 1.0)
    low = base + extent * m * (jnp.minimum(c, 0.0) + jnp.minimum(s, 0.0)) - b * 0.5
    start = jnp.floor(jnp.where(sub, low, (low - 0.25) * 0.25))
    whole[...] = start.astype(jnp.int32)
    values = g * (base - start - 0.5)
    for k, value in enumerate((g * m * c, g * m * s, g, g * jnp.minimum(b, 1.0),
                               g * (b + 1.0) * 0.5, 2.5 * s, R_SLAB / CZ * m / 1.65)):
        values = jnp.where(lane == SUBS + k, value, values)
    real[...] = values


def kernel(angles, vol_ref, mask_ref, out_ref,
           real_v, whole_v, real, whole, own_v, pair_v, own_h, pair_h, wts, res40, res32, axial_rows,
           send0, send1, send2, send3, recv0, recv1, recv2, recv3, summed, arrived,
           table_sem, vol_send, vol_recv, msg_send, msg_recv, sum_send, sum_recv):
    tile = lax.axis_index("tile")
    slab = lax.axis_index("slab")
    core = lax.rem(tile, 2)
    chip = lax.div(tile, 2)
    zh = lax.rem(chip, NZH)
    block = lax.div(chip, NZH)
    x = lax.div(block, NY)
    y = lax.rem(block, NY)
    sends = (send0, send1, send2, send3)
    recvs = (recv0, recv1, recv2, recv3)

    def device(bx, z, k):
        return (bx * NZH + z) * 2 + k

    partner = 2 * chip + 1 - core
    greeted = [(partner, slab), (tile, 1 - slab), (partner, 1 - slab)]
    for dx in range(NX):
        for dy in range(NY):
            if dx or dy:
                there = lax.rem(x + dx, NX) * NY + lax.rem(y + dy, NY)
                greeted.append((device(there, zh, core), slab))
    for dz in range(1, NZH):
        greeted.append((device(block, lax.rem(zh + dz, NZH), core), slab))
    barrier = pltpu.get_barrier_semaphore()
    for where_to in greeted:
        pl.semaphore_signal(barrier, inc=1, device_id=where_to, device_id_type=MESH)

    own_v[...] = vol_ref[...].astype(F32) * mask_ref[...].astype(F32)
    pl.semaphore_wait(barrier, len(greeted))

    edge = pl.ds(pl.multiple_of((1 - slab) * (CZ - HALO_Z), HALO_Z), HALO_Z)
    give_pair = pltpu.make_async_remote_copy(
        own_v, pair_v, vol_send.at[0], vol_recv.at[0],
        device_id=(partner, slab), device_id_type=MESH)
    give_edge = pltpu.make_async_remote_copy(
        own_v.at[edge], own_h, vol_send.at[1], vol_recv.at[1],
        device_id=(tile, 1 - slab), device_id_type=MESH)
    give_cross = pltpu.make_async_remote_copy(
        own_v.at[edge], pair_h, vol_send.at[2], vol_recv.at[2],
        device_id=(partner, 1 - slab), device_id_type=MESH)
    give_edge.start()
    give_cross.start()
    give_pair.start()
    fill_tables(angles, tile, zh, block, core, real_v, whole_v)
    to_real = pltpu.make_async_copy(real_v, real, table_sem.at[0])
    to_whole = pltpu.make_async_copy(whole_v, whole, table_sem.at[1])
    to_real.start()
    to_whole.start()
    for res, win in ((res40, 40), (res32, 32)):
        pad = 2 * win

        def clear(j, carry, res=res, win=win, pad=pad):
            res[j, 0:pad, :] = jnp.zeros((pad, 128), F32)
            res[j, pad + win:, :] = jnp.zeros((pad, 128), F32)
            return carry

        lax.fori_loop(0, NY * SUBS, clear, 0)
    for zz in range(NZH):

        def clear(j, carry, zz=zz):
            recvs[zz][j, 0:PAD, :] = jnp.zeros((PAD, 128), F32)
            recvs[zz][j, PAD + SENT_ROWS[zz]:, :] = jnp.zeros((RECV_ROWS[zz] - PAD - SENT_ROWS[zz], 128), F32)
            return carry

        lax.fori_loop(0, BLOCKS, clear, 0)


    def take_tile(k, big, halo):
        for pb in range(16):
            cols = slice(pb * 128, (pb + 1) * 128)
            part = jnp.concatenate(
                [big[:, cols], halo[:, cols], jnp.zeros((128 - CZ - HALO_Z, 128), F32)], axis=0)
            turned = part.T.astype(BF16)
            for x2 in range(2):
                xb, xi = divmod(pb * 2 + x2, SUB)
                for yb in range(4):
                    rows = slice(x2 * 64 + yb * SUB, x2 * 64 + yb * SUB + SUB)
                    wts[k * 8 + xb * 4 + yb, xi * SUB:(xi + 1) * SUB, :] = turned[rows]

    to_real.wait()
    to_whole.wait()
    give_edge.wait()
    take_tile(0, own_v, own_h)
    give_cross.wait()
    give_pair.wait()
    take_tile(1, pair_v, pair_h)

    pix = lax.broadcasted_iota(jnp.int32, (8, SUB * SUB), 1)
    pix_x = lax.div(pix, SUB).astype(F32)
    pix_y = lax.rem(pix, SUB).astype(F32)
    lane = lax.broadcasted_iota(jnp.int32, (80, 128), 1)
    zrow = lax.broadcasted_iota(jnp.int32, (80, 128), 0)
    row_low = (lax.rem(lane, R_SLAB) + slab * R_SLAB).astype(F32)
    slice_id = jnp.where(
        zrow < CZ, zrow + slab * CZ,
        jnp.where(slab == 0, zrow, zrow - HALO_Z)).astype(F32)
    z_pos = slice_id + (0.5 - CZ)

    def to_block(turn, j):
        return lax.rem(x + j, NX) * NY + lax.rem(y + j + turn, NY)

    def project(zz, dx):
        win, msg = WIN_ROWS[zz], MSG_ROWS[zz]
        res = res40 if win == 40 else res32
        pad = 2 * win
        half = 2 * msg
        krow = lax.broadcasted_iota(jnp.int32, (win, SUB * SUB), 0).astype(F32)
        ids = [zz * BLOCKS + to_block(dx, dy) for dy in range(NY)]
        pre = []
        for v in ids:
            line = real[v, SUBS] * pix_x + real[v, SUBS + 1] * pix_y
            pre.append(
                jnp.concatenate([line] * (win // 8), axis=0) - real[v, SUBS + 2] * krow)
        for i in range(SUBS):
            parts = []
            for dy, v in enumerate(ids):
                dist = jnp.abs(pre[dy] + real[v, i])
                parts.append(jnp.minimum(real[v, SUBS + 4] - dist, real[v, SUBS + 3]))
            foot = jnp.maximum(jnp.concatenate(parts, axis=0).astype(BF16), jnp.zeros((), BF16))
            got = jnp.dot(foot, wts[i], preferred_element_type=F32)
            for dy in range(NY):
                res[dy * SUBS + i, pad:pad + win, :] = got[dy * win:(dy + 1) * win]
        for dy, v in enumerate(ids):
            chunks = []
            base = pad + 4 * whole[v, SUBS]
            for ch in range(2):
                total = None
                for i in range(SUBS):
                    at = base + ch * half - whole[v, i]
                    at = jnp.minimum(jnp.maximum(at, 0), pad + win)
                    term = res[dy * SUBS + i, pl.ds(at, half), :]
                    total = term if total is None else total + term
                chunks.append(total)
            part = jnp.concatenate(chunks, axis=0)
            high = part.astype(BF16)
            low = (part - high.astype(F32)).astype(BF16)
            h, e = real[v, SUBS + 5], real[v, SUBS + 6]
            centre = (R_SLAB + h) + e * z_pos
            axial = jnp.maximum(
                jnp.minimum(centre + e * 0.5, row_low + 1.0)
                - jnp.maximum(centre - e * 0.5, row_low), 0.0)
            a_high = axial.astype(BF16)
            a_low = (axial - a_high.astype(F32)).astype(BF16)
            blank = jnp.zeros((48, 128), BF16)
            a_high = jnp.concatenate([a_high, blank], axis=0)
            a_low = jnp.concatenate([a_low, blank], axis=0)
            both = jnp.concatenate([a_high, a_low], axis=1)
            rows = jnp.dot(jnp.concatenate([high, low], axis=1),
                           jnp.concatenate([both, both], axis=0), preferred_element_type=F32)
            axial_rows[dy, 0:4 * msg, :] = rows[:, :128] + rows[:, 128:]
            quarter = lax.broadcasted_iota(jnp.int32, (msg, 128), 1)
            packed = axial_rows[dy, pl.ds(3, msg, stride=4), :]
            for q in (2, 1, 0):
                packed = jnp.where(quarter < 32 * (q + 1), axial_rows[dy, pl.ds(q, msg, stride=4), :], packed)
            sends[zz][dx * NY + dy] = packed
            away = message(zz, dx, dy)
            if dy == 0:
                @pl.when(dx == 0)
                def _():
                    keep(zz).start()

                @pl.when(dx != 0)
                def _():
                    away.start()
            else:
                away.start()

    def message(zz, dx, dy):
        there = to_block(dx, dy)
        return pltpu.make_async_remote_copy(
            sends[zz].at[dx * NY + dy, pl.ds(0, SENT_ROWS[zz])],
            recvs[zz].at[block, pl.ds(PAD, SENT_ROWS[zz])],
            msg_send.at[zz, dx * NY + dy], msg_recv.at[zz, block],
            device_id=(device(there, zh, core), slab), device_id_type=MESH)

    def keep(zz):
        return pltpu.make_async_copy(
            sends[zz].at[0, pl.ds(0, SENT_ROWS[zz])], recvs[zz].at[block, pl.ds(PAD, SENT_ROWS[zz])],
            msg_recv.at[zz, block])

    def arrival(zz, src):
        return pltpu.make_async_remote_copy(
            sends[zz].at[0, pl.ds(0, SENT_ROWS[zz])], recvs[zz].at[src, pl.ds(PAD, SENT_ROWS[zz])],
            msg_send.at[zz, 0], msg_recv.at[zz, src],
            device_id=(device(src, zh, core), slab), device_id_type=MESH)

    def total_out(zz):
        return pltpu.make_async_remote_copy(
            summed.at[zz], arrived.at[zh], sum_send.at[zz], sum_recv.at[zh],
            device_id=(device(block, zz, core), slab), device_id_type=MESH)

    def total_keep(zz):
        return pltpu.make_async_copy(summed.at[zz], arrived.at[zh], sum_recv.at[zh])

    def gather_block(zz):
        msg = MSG_ROWS[zz]

        def await_one(src, carry):
            @pl.when(src == block)
            def _():
                keep(zz).wait()

            @pl.when(src != block)
            def _():
                arrival(zz, src).wait_recv()
            return carry

        lax.fori_loop(0, BLOCKS, await_one, 0)
        for ch in range(4):
            total = None
            for src in range(BLOCKS):
                at = PAD + PAD * ch - whole[64 + zz, SUBS + src]
                at = jnp.minimum(jnp.maximum(at, 0), PAD + msg)
                term = recvs[zz][src, pl.ds(at, PAD), :]
                total = term if total is None else total + term
            summed[zz, ch * PAD:(ch + 1) * PAD, :] = total

        @pl.when(zh == zz)
        def _():
            total_keep(zz).start()

        @pl.when(zh != zz)
        def _():
            total_out(zz).start()

    for zz in range(NZH):
        def step(dx, carry, zz=zz):
            project(zz, dx)
            return carry

        lax.fori_loop(0, NX, step, 0)
        if zz:
            gather_block(zz - 1)
    gather_block(NZH - 1)

    def await_total(src, carry):
        @pl.when(src == zh)
        def _():
            total_keep(src).wait()

        @pl.when(src != zh)
        def _():
            pltpu.make_async_remote_copy(
                summed.at[0], arrived.at[src], sum_send.at[0], sum_recv.at[src],
                device_id=(device(block, src, core), slab), device_id_type=MESH).wait_recv()
            total_out(src).wait_send()
        return carry

    lax.fori_loop(0, NZH, await_total, 0)
    out_ref[...] = (arrived[0] + arrived[1]) + (arrived[2] + arrived[3])
    for zz in range(NZH):
        def drain(n, carry, zz=zz):
            message(zz, lax.div(n, NY), lax.rem(n, NY)).wait_send()
            return carry

        lax.fori_loop(1, BLOCKS, drain, 0)


def on_device(volume, fov_mask, block_angles, row_range):
    tile_id = lax.axis_index("tile")
    slab_id = lax.axis_index("slab")
    smem = pl.BlockSpec(memory_space=pltpu.SMEM)
    vmem = pl.BlockSpec(memory_space=pltpu.VMEM)
    packed = pl.pallas_call(
        kernel,
        out_shape=jax.ShapeDtypeStruct((COLS // 4, 128), F32),
        in_specs=[smem] + [vmem] * 2,
        out_specs=vmem,
        scratch_shapes=[
            pltpu.VMEM((72, 128), F32),
            pltpu.VMEM((72, 128), jnp.int32),
            pltpu.SMEM((72, 128), F32),
            pltpu.SMEM((72, 128), jnp.int32),
            pltpu.VMEM((CZ, TX * TY), F32),
            pltpu.VMEM((CZ, TX * TY), F32),
            pltpu.VMEM((HALO_Z, TX * TY), F32),
            pltpu.VMEM((HALO_Z, TX * TY), F32),
            pltpu.VMEM((SUBS, SUB * SUB, 128), BF16),
            pltpu.VMEM((NY * SUBS, 200, 128), F32),
            pltpu.VMEM((NY * SUBS, 160, 128), F32),
            pltpu.VMEM((NY, 160, 128), F32),
            *[pltpu.VMEM((BLOCKS, r, 128), F32) for r in MSG_ROWS],
            *[pltpu.VMEM((BLOCKS, r, 128), F32) for r in RECV_ROWS],
            pltpu.VMEM((NZH, COLS // 4, 128), F32),
            pltpu.VMEM((NZH, COLS // 4, 128), F32),
            pltpu.SemaphoreType.DMA((2,)),
            pltpu.SemaphoreType.DMA((3,)),
            pltpu.SemaphoreType.DMA((3,)),
            pltpu.SemaphoreType.DMA((NZH, BLOCKS)),
            pltpu.SemaphoreType.DMA((NZH, BLOCKS)),
            pltpu.SemaphoreType.DMA((NZH,)),
            pltpu.SemaphoreType.DMA((NZH,)),
        ],
        compiler_params=pltpu.CompilerParams(
            collective_id=0, has_side_effects=True, vmem_limit_bytes=52 * 1024 * 1024),
        cost_estimate=pl.CostEstimate(
            flops=64 * 16 * 40 * 256 * 128 * 2, bytes_accessed=1 << 20, transcendentals=0),
    )(block_angles, volume[0], fov_mask)
    rows = packed.reshape(COLS // 4, 4, R_SLAB).transpose(2, 0, 1).reshape(R_SLAB, COLS)
    global_rows = slab_id * R_SLAB + jnp.arange(R_SLAB, dtype=jnp.int32)
    in_range = (global_rows >= row_range[tile_id, 0]) & (global_rows < row_range[tile_id, 1])
    return jnp.where(in_range[:, None], rows, F32(0.0))[None]


def solution(mesh):
    in_specs = (P("tile", "slab", None), P("tile", None), P(), P())
    out_specs = P("tile", "slab", None)
    return jax.shard_map(
        on_device, mesh=mesh, in_specs=in_specs, out_specs=out_specs, check_vma=False
    )
```

time: 74.6 us -> 60 us (0.80)
  other arithmetic: 11.8 us -> 1.32 us
  local copies, waits for them, and re-layouts: 7.14 us -> 3.38 us
    cos x2 -> x0, other arithmetic: 10.1 us -> none  [view_geometry(): cos_part = jnp.cos(angle_rad)]
    gather x2 -> x0, local copies, waits for them, and re-layouts: 1.49 us -> none  [view_geometry(): angle_index = block_angles[view_id // 8] + 150 * (view_id % 8)]
    unnamed x9 -> x8, local copies, waits for them, and re-layouts: 2.06 us -> 1.63 us
where the time goes in v2:
time: 60 us; the launch traced here: 59.8 us
  Pallas kernels  55.1 us (92%)
  local copies, waits for them, and re-layouts  3.38 us (6%)
  other arithmetic  1.32 us (2%)
    pallas_call x1, Pallas kernels, on_device(): pl.pallas_call(kernel, out_shape=jax.ShapeDtypeStruct((COLS // 4, 128), F...  55.1 us
    unnamed x8, local copies, waits for them, and re-layouts  1.63 us
    and x1, other arithmetic, on_device(): (global_rows >= row_range[tile_id, 0]) & (global_rows < row_range[tile_id...  1.28 us

profile of v2, /device:TPU:1, one launch (start us, length us, event | category | flops | bytes accessed | tf_op | source)
XLA Modules:
  0.0 59.8 jit_solution(17629556946495425255)
XLA Ops:
  0.0 0.0 copy-start.3
  0.0 0.0 copy-start.1
  0.0 0.7 %copy-done.3 = s32[128,2]{0,1:T(2,128)S(1)} copy-done((s32[128,2]{0,1:T(2,128)S(1)}, s32[128,2]{0,1:T(2,128)}, u32[]{:S(2)}) %copy-start.3) | copy-done | bytes 1048
  0.7 0.6 constant_dynamic-slice_fusion.1
  1.3 0.0 copy-start.2
  1.3 1.3 %compare_and_fusion = pred[32]{0:T(512)(128)(4,1)S(1)} fusion(s32[]{:T(128)} %bitcast.1, s32[]{:T(128)} %bitcast, s32[]{:T(128)S(6)} %mul.3), kind=kLoop, calls=%fused_computation.1 | loop fusion | flops 128 | bytes 44 | tf_op jit(solution)/shard_map/and | solution.py:376
  2.6 0.0 copy-done.1
  2.6 0.0 copy-done.2
  2.6 0.0 copy-start
  2.6 0.9 %copy-done = bf16[1,64,2048]{2,1,0:T(8,128)(2,1)S(1)} copy-done((bf16[1,64,2048]{2,1,0:T(8,128)(2,1)S(1)}, bf16[1,64,2048]{2,1,0:T(8,128)(2,1)}, u32[]{:S(2)}) %copy-start) | copy-done | bytes 262168
  3.5 55.1 %shard_map.46 = f32[256,128]{1,0:T(8,128)S(1)} custom-call(s32[16]{0:T(128)S(1)} %copy-done.2, bf16[64,2048]{1,0:T(8,128)(2,1)S(1)} %bitcast.7, s32[1,2048]{1,0:T(1,128)S(1)} %copy-done.1), custom_call_target="tpu_custom_call" | custom-call | flops 2684354560 | bytes 1048576 | tf_op jit(solution)/shard_map/pallas_call | solution.py:339
  58.6 0.1 copy.6
  58.7 0.2 copy.7
  59.0 0.8 %copy.8 = f32[1,32,1024]{2,1,0:T(8,128)} copy(f32[1,32,1024]{1,2,0:T(8,128)S(1)} %broadcast_select_fusion) | data formatting | bytes 262144 | tf_op jit(solution)/shard_map/jit(_where)/select_n | solution.py:377
  (1 shorter events, 0.0 us)
Async XLA Ops:
  0.0 0.7 %copy-start.3 = (s32[128,2]{0,1:T(2,128)S(1)}, s32[128,2]{0,1:T(2,128)}, u32[]{:S(2)}) copy-start(s32[128,2]{0,1:T(2,128)} %param.7) | copy-start | bytes 3076
  0.0 2.6 %copy-start.1 = (s32[1,2048]{1,0:T(1,128)S(1)}, s32[1,2048]{1,0:T(1,128)}, u32[]{:S(2)}) copy-start(s32[1,2048]{1,0:T(1,128)} %mask_ref.1) | copy-start | bytes 24580
  1.3 1.3 %copy-start.2 = (s32[16]{0:T(128)S(1)}, s32[16]{0:T(128)}, u32[]{:S(2)}) copy-start(s32[16]{0:T(128)} %angles.1) | copy-start | bytes 196
  2.6 1.0 %copy-start = (bf16[1,64,2048]{2,1,0:T(8,128)(2,1)S(1)}, bf16[1,64,2048]{2,1,0:T(8,128)(2,1)}, u32[]{:S(2)}) copy-start(bf16[1,64,2048]{2,1,0:T(8,128)(2,1)} %param.4) | copy-start | bytes 786436

commit v3 on v2

v3 whole, which is shorter than its diff:
```python
import math

import jax
import jax.numpy as jnp
from jax import lax
from jax.experimental import pallas as pl
from jax.experimental.pallas import tpu as pltpu
from jax.sharding import PartitionSpec as P

COLS = 1024
R_SLAB = 32
TX = 32
TY = 64
GRID_X = 16
CZ = 64
SUB = 16
NX = 4
NY = 4
NZH = 4
BLOCKS = NX * NY
SUBS = 16
HALO_Z = 8
F32 = jnp.float32
BF16 = jnp.bfloat16
MESH = pl.DeviceIdType.MESH
WIN_ROWS = (40, 32)
MSG_ROWS = (40, 32)
SENT_ROWS = (37, 26)
LAND = 40
PAD = 64
RES_PAD = 80


def fill_tables(angles, tile, zh, block, core, real, whole):
    shape = (72, 128)
    row = lax.broadcasted_iota(jnp.int32, shape, 0)
    lane = lax.broadcasted_iota(jnp.int32, shape, 1)
    own = row < 64
    zz = jnp.where(own, row >> 4, row & 3)
    angle = jnp.zeros(shape, jnp.int32) + angles[block]
    for k in range(BLOCKS):
        angle = jnp.where(own & ((row & 15) == k), angles[k], angle)
    angle = angle + 150 * (2 * zz + core)
    theta = angle.astype(F32) * (2.0 * math.pi / 1200.0)
    c, s = jnp.cos(theta), jnp.sin(theta)
    spread = jnp.maximum(jnp.abs(c), jnp.abs(s))
    m = 1.3 + 0.35 * c
    b = m * spread
    g = 1.0 / spread
    backward = jnp.minimum(c, 0.0) + jnp.minimum(s, 0.0)

    def corner(tiles, mirror, off_x, off_y):
        along = tiles & 15
        grow = tiles >> 4
        gcol = jnp.where((grow & 1) == 1, mirror - along, along)
        px = (gcol * TX + off_x).astype(F32) + (0.5 - GRID_X * TX / 2)
        py = (grow * TY + off_y).astype(F32) + (0.5 - 128 // GRID_X * TY / 2)
        return COLS / 2 + m * (px * c + py * s)

    group = lane >> 4
    i = lane & 15
    base = corner(jnp.where(i < 8, tile, tile + 1 - 2 * core), 15,
                  ((i >> 2) & 1) * SUB, (i & 3) * SUB)
    start = jnp.floor(base + (SUB - 1.0) * m * backward - b * 0.5)
    origin = corner(jnp.where(own, tile - core, (i * NZH + zh) * 2), 14, 0, 0)
    low = origin + (4.0 * SUB - 1.0) * m * backward - b * 0.5
    first4 = jnp.floor((low - 0.25) * 0.25).astype(jnp.int32)
    msg = jnp.where((zz == 1) | (zz == 2), MSG_ROWS[1], MSG_ROWS[0])
    at = RES_PAD + 4 * first4 - start.astype(jnp.int32) + group * 2 * msg
    at = jnp.minimum(jnp.maximum(at, 0), RES_PAD + WIN_ROWS[0])
    come = jnp.minimum(jnp.maximum(PAD + PAD * (group & 3) - first4, 0), PAD + LAND)
    whole[...] = jnp.where(own, at, come)
    values = g * (base - start - 0.5)
    for k, value in enumerate((g * m * c, g * m * s, g, g * jnp.minimum(b, 1.0),
                               g * (b + 1.0) * 0.5, 2.5 * s, R_SLAB / CZ * m / 1.65)):
        values = jnp.where(lane == SUBS + k, value, values)
    real[...] = values


def kernel(angles, limits, vol_hbm, mask_hbm, out_ref,
           vol_ref, mask_ref, real_v, whole_v, real, whole, own_v, pair_v, own_h, pair_h,
           wts, res_a, res_b, axial_rows, sends, lands, spread, summed, arrived,
           in_sem, table_sem, vol_send, vol_recv, msg_send, msg_recv, sum_send, sum_recv):
    tile = lax.axis_index("tile")
    slab = lax.axis_index("slab")
    core = lax.rem(tile, 2)
    chip = lax.div(tile, 2)
    zh = lax.rem(chip, NZH)
    block = lax.div(chip, NZH)
    x = lax.div(block, NY)
    y = lax.rem(block, NY)
    get_vol = pltpu.make_async_copy(vol_hbm.at[0], vol_ref, in_sem.at[0])
    get_mask = pltpu.make_async_copy(mask_hbm, mask_ref, in_sem.at[1])
    get_vol.start()
    get_mask.start()

    def flipped(turn):
        mask = lax.rem(turn + 1, 4)
        high = lax.rem(lax.div(zh, 2) + lax.div(mask, 2), 2)
        low = lax.rem(lax.rem(zh, 2) + lax.rem(mask, 2), 2)
        return 2 * high + low

    def device(bx, z, k):
        return (bx * NZH + z) * 2 + k

    partner = 2 * chip + 1 - core
    greeted = [(partner, slab), (tile, 1 - slab), (partner, 1 - slab)]
    for dx in range(NX):
        for dy in range(NY):
            if dx or dy:
                there = lax.rem(x + dx, NX) * NY + lax.rem(y + dy, NY)
                greeted.append((device(there, zh, core), slab))
    for turn in range(NZH - 1):
        greeted.append((device(block, flipped(turn), core), slab))
    barrier = pltpu.get_barrier_semaphore()
    for where_to in greeted:
        pl.semaphore_signal(barrier, inc=1, device_id=where_to, device_id_type=MESH)

    get_vol.wait()
    get_mask.wait()
    own_v[...] = vol_ref[...].astype(F32) * mask_ref[...].astype(F32)
    pl.semaphore_wait(barrier, len(greeted))

    edge = pl.ds(pl.multiple_of((1 - slab) * (CZ - HALO_Z), HALO_Z), HALO_Z)
    give_pair = pltpu.make_async_remote_copy(
        own_v, pair_v, vol_send.at[0], vol_recv.at[0],
        device_id=(partner, slab), device_id_type=MESH)
    give_edge = pltpu.make_async_remote_copy(
        own_v.at[edge], own_h, vol_send.at[1], vol_recv.at[1],
        device_id=(tile, 1 - slab), device_id_type=MESH)
    give_cross = pltpu.make_async_remote_copy(
        own_v.at[edge], pair_h, vol_send.at[2], vol_recv.at[2],
        device_id=(partner, 1 - slab), device_id_type=MESH)
    give_edge.start()
    give_cross.start()
    give_pair.start()
    fill_tables(angles, tile, zh, block, core, real_v, whole_v)
    to_real = pltpu.make_async_copy(real_v, real, table_sem.at[0])
    to_whole = pltpu.make_async_copy(whole_v, whole, table_sem.at[1])
    to_real.start()
    to_whole.start()
    for res in (res_a, res_b):

        def clear(j, carry, res=res):
            res[j, 0:RES_PAD, :] = jnp.zeros((RES_PAD, 128), F32)
            res[j, RES_PAD + 32:, :] = jnp.zeros((RES_PAD + 8, 128), F32)
            return carry

        lax.fori_loop(0, 2 * SUBS, clear, 0)
    def clear(j, carry):
        spread[j, 0:PAD, :] = jnp.zeros((PAD, 128), F32)
        spread[j, PAD + LAND:, :] = jnp.zeros((PAD, 128), F32)
        for zz in range(NZH):
            sent = SENT_ROWS[int(zz in (1, 2))]
            lands[zz, j, sent:LAND, :] = jnp.zeros((LAND - sent, 128), F32)
        return carry

    lax.fori_loop(0, BLOCKS, clear, 0)
    def take_tile(k, big, halo):
        for pb in range(16):
            cols = slice(pb * 128, (pb + 1) * 128)
            part = jnp.concatenate(
                [big[:, cols], halo[:, cols], jnp.zeros((128 - CZ - HALO_Z, 128), F32)], axis=0)
            turned = part.T.astype(BF16)
            for x2 in range(2):
                xb, xi = divmod(pb * 2 + x2, SUB)
                for yb in range(4):
                    rows = slice(x2 * 64 + yb * SUB, x2 * 64 + yb * SUB + SUB)
                    wts[k * 8 + xb * 4 + yb, xi * SUB:(xi + 1) * SUB, :] = turned[rows]

    to_real.wait()
    to_whole.wait()
    give_edge.wait()
    take_tile(0, own_v, own_h)
    give_cross.wait()
    give_pair.wait()
    take_tile(1, pair_v, pair_h)

    pix = lax.broadcasted_iota(jnp.int32, (8, SUB * SUB), 1)
    pix_x = lax.div(pix, SUB).astype(F32)
    pix_y = lax.rem(pix, SUB).astype(F32)
    lane = lax.broadcasted_iota(jnp.int32, (80, 128), 1)
    zrow = lax.broadcasted_iota(jnp.int32, (80, 128), 0)
    row_low = (lax.rem(lane, R_SLAB) + slab * R_SLAB).astype(F32)
    slice_id = jnp.where(
        zrow < CZ, zrow + slab * CZ,
        jnp.where(slab == 0, zrow, zrow - HALO_Z)).astype(F32)
    z_pos = slice_id + (0.5 - CZ)

    def to_block(turn, j):
        return lax.rem(x + j, NX) * NY + lax.rem(y + j + turn, NY)

    def views(zz, turn, half):
        return [zz * BLOCKS + to_block(turn, j) for j in (2 * half, 2 * half + 1)]

    def footprints(kind, zz, turn, half, res):
        win = WIN_ROWS[kind]
        ids = views(zz, turn, half)
        krow = lax.broadcasted_iota(jnp.int32, (win, SUB * SUB), 0).astype(F32)
        pre, caps = [], []
        for v in ids:
            line = real[v, SUBS] * pix_x + real[v, SUBS + 1] * pix_y
            pre.append(
                jnp.concatenate([line] * (win // 8), axis=0) - real[v, SUBS + 2] * krow)
            caps.append(jnp.full((win, SUB * SUB), real[v, SUBS + 3], F32))
        cap = jnp.concatenate(caps, axis=0).astype(BF16)
        for i in range(SUBS):
            parts = []
            for k, v in enumerate(ids):
                parts.append(real[v, SUBS + 4] - jnp.abs(pre[k] + real[v, i]))
            foot = jnp.concatenate(parts, axis=0).astype(BF16)
            foot = jnp.maximum(jnp.minimum(foot, cap), jnp.zeros((), BF16))
            got = jnp.dot(foot, wts[i], preferred_element_type=F32)
            for k in range(2):
                res[k * SUBS + i, RES_PAD:RES_PAD + win, :] = got[k * win:(k + 1) * win]
                if win < WIN_ROWS[0]:
                    res[k * SUBS + i, RES_PAD + win:RES_PAD + WIN_ROWS[0], :] = jnp.zeros(
                        (WIN_ROWS[0] - win, 128), F32)
            yield

    def messages(kind, zz, turn, half, res):
        msg = MSG_ROWS[kind]
        reach = 2 * msg
        for k, v in enumerate(views(zz, turn, half)):
            chunks = []
            for ch in range(2):
                total = None
                for i in range(SUBS):
                    term = res[k * SUBS + i, pl.ds(whole[v, ch * SUBS + i], reach), :]
                    total = term if total is None else total + term
                    if i % 5 == 4:
                        yield
                chunks.append(total)
            part = jnp.concatenate(chunks, axis=0)
            high = part.astype(BF16)
            low = (part - high.astype(F32)).astype(BF16)
            h, e = real[v, SUBS + 5], real[v, SUBS + 6]
            centre = (R_SLAB + h) + e * z_pos
            axial = jnp.maximum(
                jnp.minimum(centre + e * 0.5, row_low + 1.0)
                - jnp.maximum(centre - e * 0.5, row_low), 0.0)
            a_high = axial.astype(BF16)
            a_low = (axial - a_high.astype(F32)).astype(BF16)
            blank = jnp.zeros((48, 128), BF16)
            a_high = jnp.concatenate([a_high, blank], axis=0)
            a_low = jnp.concatenate([a_low, blank], axis=0)
            both = jnp.concatenate([a_high, a_low], axis=1)
            rows = jnp.dot(jnp.concatenate([high, low], axis=1),
                           jnp.concatenate([both, both], axis=0), preferred_element_type=F32)
            at = 2 * half + k
            axial_rows[at, 0:4 * msg, :] = rows[:, :128] + rows[:, 128:]
            yield
            quarter = lax.broadcasted_iota(jnp.int32, (msg, 128), 1)
            packed = axial_rows[at, pl.ds(3, msg, stride=4), :]
            for q in (2, 1, 0):
                packed = jnp.where(
                    quarter < 32 * (q + 1), axial_rows[at, pl.ds(q, msg, stride=4), :], packed)
            sends[zz, turn * NY + at, 0:msg, :] = packed
            yield

    def together(*works):
        works = list(works)
        while works:
            for work in list(works):
                if next(work, works) is works:
                    works.remove(work)

    def message(kind, zz, turn, j):
        rows = SENT_ROWS[kind]
        return pltpu.make_async_remote_copy(
            sends.at[zz, turn * NY + j, pl.ds(0, rows)], lands.at[zz, block, pl.ds(0, rows)],
            msg_send.at[zz, turn * NY + j], msg_recv.at[zz, block],
            device_id=(device(to_block(turn, j), zh, core), slab), device_id_type=MESH)

    def keep(kind, zz):
        rows = SENT_ROWS[kind]
        return pltpu.make_async_copy(
            sends.at[zz, 0, pl.ds(0, rows)], lands.at[zz, block, pl.ds(0, rows)],
            msg_recv.at[zz, block])

    def arrival(kind, zz, src):
        rows = SENT_ROWS[kind]
        return pltpu.make_async_remote_copy(
            sends.at[zz, 0, pl.ds(0, rows)], lands.at[zz, src, pl.ds(0, rows)],
            msg_send.at[zz, 0], msg_recv.at[zz, src],
            device_id=(device(src, zh, core), slab), device_id_type=MESH)

    def total_out(turn):
        return pltpu.make_async_remote_copy(
            summed.at[turn], arrived.at[turn], sum_send.at[turn], sum_recv.at[turn],
            device_id=(device(block, flipped(turn), core), slab), device_id_type=MESH)

    def octant(kind, zz):
        def step(turn, carry):
            before = jnp.maximum(turn - 1, 0)
            together(footprints(kind, zz, turn, 0, res_a), messages(kind, zz, before, 1, res_b))

            @pl.when(turn > 0)
            def _():
                message(kind, zz, turn - 1, 2).start()
                message(kind, zz, turn - 1, 3).start()

            together(footprints(kind, zz, turn, 1, res_b), messages(kind, zz, turn, 0, res_a))

            @pl.when(turn == 0)
            def _():
                keep(kind, zz).start()

            @pl.when(turn > 0)
            def _():
                message(kind, zz, turn, 0).start()

            message(kind, zz, turn, 1).start()
            return carry

        lax.fori_loop(0, NX, step, 0)
        together(messages(kind, zz, NX - 1, 1, res_b))
        message(kind, zz, NX - 1, 2).start()
        message(kind, zz, NX - 1, 3).start()

    def by_kind(zz, work):
        narrow = (zz == 1) | (zz == 2)

        @pl.when(narrow)
        def _():
            work(1)

        @pl.when(jnp.logical_not(narrow))
        def _():
            work(0)

    def gather_block(turn):
        zz = flipped(turn)

        def await_all(kind):
            def await_one(src, carry):
                @pl.when(src == block)
                def _():
                    keep(kind, zz).wait()

                @pl.when(src != block)
                def _():
                    arrival(kind, zz, src).wait_recv()
                return carry

            lax.fori_loop(0, BLOCKS, await_one, 0)

        by_kind(zz, await_all)
        for src in range(BLOCKS):
            spread[src, PAD:PAD + LAND, :] = lands[zz, src]
        for ch in range(4):
            total = None
            for src in range(BLOCKS):
                term = spread[src, pl.ds(whole[64 + zz, 64 + ch * BLOCKS + src], PAD), :]
                total = term if total is None else total + term
            summed[turn, ch * PAD:(ch + 1) * PAD, :] = total

    def one_octant(turn, carry):
        zz = flipped(turn)
        by_kind(zz, lambda kind: octant(kind, zz))

        @pl.when(turn > 0)
        def _():
            gather_block(turn - 1)
            total_out(turn - 1).start()
        return carry

    lax.fori_loop(0, NZH, one_octant, 0)
    gather_block(NZH - 1)
    for turn in range(NZH - 1):
        total_out(turn).wait()
    out_row = lax.rem(lax.broadcasted_iota(jnp.int32, (COLS // 4, 128), 1), R_SLAB) + slab * R_SLAB
    read_out = (out_row >= limits[tile, 0]) & (out_row < limits[tile, 1])
    total = (arrived[0] + arrived[1]) + (arrived[2] + summed[NZH - 1])
    out_ref[...] = jnp.where(read_out, total, 0.0)
    for zz in range(NZH):
        def drain(n, carry, zz=zz):
            message(int(zz in (1, 2)), zz, lax.div(n, NY), lax.rem(n, NY)).wait_send()
            return carry

        lax.fori_loop(1, BLOCKS, drain, 0)


def on_device(volume, fov_mask, block_angles, row_range):
    smem = pl.BlockSpec(memory_space=pltpu.SMEM)
    anywhere = pl.BlockSpec(memory_space=pl.ANY)
    pixels = TX * TY
    packed = pl.pallas_call(
        kernel,
        out_shape=jax.ShapeDtypeStruct((COLS // 4, 128), F32),
        in_specs=[smem, smem, anywhere, anywhere],
        out_specs=pl.BlockSpec(memory_space=pltpu.VMEM),
        scratch_shapes=[
            pltpu.VMEM((CZ, pixels), BF16),
            pltpu.VMEM((1, pixels), jnp.int32),
            pltpu.VMEM((72, 128), F32),
            pltpu.VMEM((72, 128), jnp.int32),
            pltpu.SMEM((72, 128), F32),
            pltpu.SMEM((72, 128), jnp.int32),
            pltpu.VMEM((CZ, pixels), F32),
            pltpu.VMEM((CZ, pixels), F32),
            pltpu.VMEM((HALO_Z, pixels), F32),
            pltpu.VMEM((HALO_Z, pixels), F32),
            pltpu.VMEM((SUBS, SUB * SUB, 128), BF16),
            pltpu.VMEM((2 * SUBS, 2 * RES_PAD + 40, 128), F32),
            pltpu.VMEM((2 * SUBS, 2 * RES_PAD + 40, 128), F32),
            pltpu.VMEM((NY, 160, 128), F32),
            pltpu.VMEM((NZH, BLOCKS, LAND, 128), F32),
            pltpu.VMEM((NZH, BLOCKS, LAND, 128), F32),
            pltpu.VMEM((BLOCKS, LAND + 2 * PAD, 128), F32),
            pltpu.VMEM((NZH, COLS // 4, 128), F32),
            pltpu.VMEM((NZH - 1, COLS // 4, 128), F32),
            pltpu.SemaphoreType.DMA((2,)),
            pltpu.SemaphoreType.DMA((2,)),
            pltpu.SemaphoreType.DMA((3,)),
            pltpu.SemaphoreType.DMA((3,)),
            pltpu.SemaphoreType.DMA((NZH, BLOCKS)),
            pltpu.SemaphoreType.DMA((NZH, BLOCKS)),
            pltpu.SemaphoreType.DMA((NZH - 1,)),
            pltpu.SemaphoreType.DMA((NZH - 1,)),
        ],
        compiler_params=pltpu.CompilerParams(
            collective_id=0, has_side_effects=True, vmem_limit_bytes=44 * 1024 * 1024),
        cost_estimate=pl.CostEstimate(
            flops=64 * 16 * 40 * 256 * 128 * 2, bytes_accessed=1 << 20, transcendentals=0),
    )(block_angles, row_range, volume, fov_mask)
    return packed.reshape(COLS // 4, 4, R_SLAB).transpose(2, 0, 1).reshape(1, R_SLAB, COLS)


def solution(mesh):
    in_specs = (P("tile", "slab", None), P("tile", None), P(), P())
    out_specs = P("tile", "slab", None)
    return jax.shard_map(
        on_device, mesh=mesh, in_specs=in_specs, out_specs=out_specs, check_vma=False
    )
```

time: 60 us -> 51.9 us (0.86)
  the two profiles are of different devices: /device:TPU:1 before, /device:TPU:33 now
where the time goes in v3:
time: 51.9 us; the launch traced here: 51.8 us
  Pallas kernels  48.8 us (94%)
  local copies, waits for them, and re-layouts  2.92 us (6%)
    pallas_call x1, Pallas kernels, on_device(): pl.pallas_call(kernel, out_shape=jax.ShapeDtypeStruct((COLS // 4, 128), F...  48.8 us
    unnamed x7, local copies, waits for them, and re-layouts  1.76 us

profile of v3, /device:TPU:33, one launch (start us, length us, event | category | flops | bytes accessed | tf_op | source)
XLA Modules:
  0.0 51.8 jit_solution(11214362735512656960)
XLA Ops:
  0.0 0.0 copy-start.2
  0.0 0.0 copy-start.1
  0.0 0.8 %copy.7.limits = s32[128,2]{1,0:T(8,128)S(1)} copy(s32[128,2]{0,1:T(2,128)} %param.7) | data formatting | bytes 2048 | tf_op args[3]
  0.8 0.0 copy-done.2
  0.8 0.0 copy-done.1
  0.8 0.0 copy-start
  0.8 0.9 %copy-done = bf16[1,64,2048]{2,1,0:T(8,128)(2,1)S(1)} copy-done((bf16[1,64,2048]{2,1,0:T(8,128)(2,1)S(1)}, bf16[1,64,2048]{2,1,0:T(8,128)(2,1)}, u32[]{:S(2)}) %copy-start) | copy-done | bytes 262168
  1.8 48.8 %shard_map.46 = f32[256,128]{1,0:T(8,128)S(1)} custom-call(s32[16]{0:T(128)S(1)} %copy-done.2, s32[128,2]{1,0:T(8,128)S(1)} %copy.7.limits, bf16[1,64,2048]{2,1,0:T(8,128)(2,1)S(1)} %copy-done, s32[1,2048]{1,0:T(1,128)S(1)} %copy-done.1), custom_call_target="tpu_custom_call" | custom-call | flops 2684354560 | bytes 1048576 | tf_op jit(solution)/shard_map/pallas_call | solution.py:388
  50.6 0.1 copy.8
  50.7 0.2 copy.9
  51.0 0.8 %copy.10 = f32[1,32,1024]{2,1,0:T(8,128)} copy(f32[1,32,1024]{1,2,0:T(8,128)S(1)} %bitcast.4) | data formatting | bytes 262144 | tf_op jit(solution)/shard_map/reshape | solution.py:427
Async XLA Ops:
  0.0 0.8 %copy-start.2 = (s32[16]{0:T(128)S(1)}, s32[16]{0:T(128)}, u32[]{:S(2)}) copy-start(s32[16]{0:T(128)} %angles.1) | copy-start | bytes 196
  0.0 0.8 %copy-start.1 = (s32[1,2048]{1,0:T(1,128)S(1)}, s32[1,2048]{1,0:T(1,128)}, u32[]{:S(2)}) copy-start(s32[1,2048]{1,0:T(1,128)} %mask_hbm.1) | copy-start | bytes 24580
  0.8 1.0 %copy-start = (bf16[1,64,2048]{2,1,0:T(8,128)(2,1)S(1)}, bf16[1,64,2048]{2,1,0:T(8,128)(2,1)}, u32[]{:S(2)}) copy-start(bf16[1,64,2048]{2,1,0:T(8,128)(2,1)} %vol_hbm.1) | copy-start | bytes 786436

commit v4 on v3

--- a/solution.py
+++ b/solution.py
@@ -2,6 +2,7 @@
 
 import jax
 import jax.numpy as jnp
+import numpy as np
 from jax import lax
 from jax.experimental import pallas as pl
 from jax.experimental.pallas import tpu as pltpu
@@ -27,8 +28,31 @@
 MSG_ROWS = (40, 32)
 SENT_ROWS = (37, 26)
 LAND = 40
+SPANS = ((0, 256), (24, 232))
 PAD = 64
-RES_PAD = 80
+RES_PAD = 120
+RES_ROWS = RES_PAD + 160
+
+
+def window_rows(kind):
+    octants = ((0, 1, 6, 7), (2, 3, 4, 5))[kind]
+    index = np.concatenate([np.arange(151) + 150 * o for o in octants])
+    c, s = np.cos(index * (2 * np.pi / 1200)), np.sin(index * (2 * np.pi / 1200))
+    m = 1.3 + 0.35 * c
+    primary = m * np.maximum(np.abs(c), np.abs(s))
+    second = m * np.minimum(np.abs(c), np.abs(s))
+    need = (15 * (primary + second) + primary).max() + 2.0
+    spans = []
+    for a in range(4):
+        for d in range(4):
+            shift = SUB * (a * primary + d * second)
+            low = max(int((shift.min() - 1.0) // 8) * 8, 0)
+            top = shift.max() + 4.5
+            high = min(-int(-(top + need) // 8) * 8, 4 * MSG_ROWS[kind])
+            assert top - low < RES_PAD and high - shift.min() + 1 < RES_PAD + 40
+            assert 0 <= low and high <= 160
+            spans.append((low, high))
+    return spans
 
 
 def fill_tables(angles, tile, zh, block, core, real, whole):
@@ -49,25 +73,29 @@
     g = 1.0 / spread
     backward = jnp.minimum(c, 0.0) + jnp.minimum(s, 0.0)
 
-    def corner(tiles, mirror, off_x, off_y):
+    def corner(tiles, off_x, off_y):
         along = tiles & 15
         grow = tiles >> 4
-        gcol = jnp.where((grow & 1) == 1, mirror - along, along)
+        gcol = jnp.where((grow & 1) == 1, 14 - along, along)
         px = (gcol * TX + off_x).astype(F32) + (0.5 - GRID_X * TX / 2)
         py = (grow * TY + off_y).astype(F32) + (0.5 - 128 // GRID_X * TY / 2)
         return COLS / 2 + m * (px * c + py * s)
 
     group = lane >> 4
     i = lane & 15
-    base = corner(jnp.where(i < 8, tile, tile + 1 - 2 * core), 15,
-                  ((i >> 2) & 1) * SUB, (i & 3) * SUB)
+    along_x = ((zz + core) & 1) == 0
+    narrow = (zz == 1) | (zz == 2)
+    step_x = jnp.where(along_x, i >> 2, i & 3)
+    step_y = jnp.where(along_x, i & 3, i >> 2)
+    step_x = jnp.where(narrow, 3 - step_x, step_x)
+    step_y = jnp.where(zz >= 2, 3 - step_y, step_y)
+    base = corner(tile - core + 0 * lane, step_x * SUB, step_y * SUB)
     start = jnp.floor(base + (SUB - 1.0) * m * backward - b * 0.5)
-    origin = corner(jnp.where(own, tile - core, (i * NZH + zh) * 2), 14, 0, 0)
+    origin = corner(jnp.where(own, tile - core, (i * NZH + zh) * 2), 0, 0)
     low = origin + (4.0 * SUB - 1.0) * m * backward - b * 0.5
     first4 = jnp.floor((low - 0.25) * 0.25).astype(jnp.int32)
-    msg = jnp.where((zz == 1) | (zz == 2), MSG_ROWS[1], MSG_ROWS[0])
-    at = RES_PAD + 4 * first4 - start.astype(jnp.int32) + group * 2 * msg
-    at = jnp.minimum(jnp.maximum(at, 0), RES_PAD + WIN_ROWS[0])
+    at = RES_PAD + 4 * first4 - start.astype(jnp.int32)
+    at = jnp.minimum(jnp.maximum(at, 0), RES_PAD)
     come = jnp.minimum(jnp.maximum(PAD + PAD * (group & 3) - first4, 0), PAD + LAND)
     whole[...] = jnp.where(own, at, come)
     values = g * (base - start - 0.5)
@@ -95,7 +123,7 @@
     get_mask.start()
 
     def flipped(turn):
-        mask = lax.rem(turn + 1, 4)
+        mask = lax.rem(lax.rem(turn + 1, 4) * 2 + lax.div(lax.rem(turn + 1, 4), 2), 4)
         high = lax.rem(lax.div(zh, 2) + lax.div(mask, 2), 2)
         low = lax.rem(lax.rem(zh, 2) + lax.rem(mask, 2), 2)
         return 2 * high + low
@@ -143,7 +171,7 @@
 
         def clear(j, carry, res=res):
             res[j, 0:RES_PAD, :] = jnp.zeros((RES_PAD, 128), F32)
-            res[j, RES_PAD + 32:, :] = jnp.zeros((RES_PAD + 8, 128), F32)
+            res[j, RES_PAD + 32:, :] = jnp.zeros((RES_ROWS - RES_PAD - 32, 128), F32)
             return carry
 
         lax.fori_loop(0, 2 * SUBS, clear, 0)
@@ -156,7 +184,7 @@
         return carry
 
     lax.fori_loop(0, BLOCKS, clear, 0)
-    def take_tile(k, big, halo):
+    def take_tile(side, big, halo):
         for pb in range(16):
             cols = slice(pb * 128, (pb + 1) * 128)
             part = jnp.concatenate(
@@ -166,29 +194,40 @@
                 xb, xi = divmod(pb * 2 + x2, SUB)
                 for yb in range(4):
                     rows = slice(x2 * 64 + yb * SUB, x2 * 64 + yb * SUB + SUB)
-                    wts[k * 8 + xb * 4 + yb, xi * SUB:(xi + 1) * SUB, :] = turned[rows]
+                    wts[(2 * side + xb) * 4 + yb, xi * SUB:(xi + 1) * SUB, :] = turned[rows]
 
     to_real.wait()
     to_whole.wait()
     give_edge.wait()
-    take_tile(0, own_v, own_h)
+    side = lax.rem(core + lax.div(tile, GRID_X), 2)
+    take_tile(side, own_v, own_h)
     give_cross.wait()
     give_pair.wait()
-    take_tile(1, pair_v, pair_h)
+    take_tile(1 - side, pair_v, pair_h)
 
     pix = lax.broadcasted_iota(jnp.int32, (8, SUB * SUB), 1)
     pix_x = lax.div(pix, SUB).astype(F32)
     pix_y = lax.rem(pix, SUB).astype(F32)
-    lane = lax.broadcasted_iota(jnp.int32, (80, 128), 1)
-    zrow = lax.broadcasted_iota(jnp.int32, (80, 128), 0)
-    row_low = (lax.rem(lane, R_SLAB) + slab * R_SLAB).astype(F32)
+    zlane = lax.broadcasted_iota(jnp.int32, (R_SLAB, 128), 1)
+    row_low = (lax.broadcasted_iota(jnp.int32, (R_SLAB, 128), 0) + slab * R_SLAB).astype(F32)
     slice_id = jnp.where(
-        zrow < CZ, zrow + slab * CZ,
-        jnp.where(slab == 0, zrow, zrow - HALO_Z)).astype(F32)
+        zlane < CZ, zlane + slab * CZ,
+        jnp.where(slab == 0, zlane, zlane - HALO_Z)).astype(F32)
     z_pos = slice_id + (0.5 - CZ)
 
     def to_block(turn, j):
         return lax.rem(x + j, NX) * NY + lax.rem(y + j + turn, NY)
+
+    def weight_of(zz, i):
+        a, d = divmod(i, 4)
+        along_x = 1 - lax.rem(zz + core, 2)
+        narrow = lax.rem(zz, 2) + lax.div(zz, 2) - 2 * lax.rem(zz, 2) * lax.div(zz, 2)
+        late = lax.div(zz, 2)
+        step_x = along_x * a + (1 - along_x) * d
+        step_y = along_x * d + (1 - along_x) * a
+        step_x = narrow * (3 - 2 * step_x) + step_x
+        step_y = late * (3 - 2 * step_y) + step_y
+        return 4 * step_x + step_y
 
     def views(zz, turn, half):
         return [zz * BLOCKS + to_block(turn, j) for j in (2 * half, 2 * half + 1)]
@@ -210,7 +249,7 @@
                 parts.append(real[v, SUBS + 4] - jnp.abs(pre[k] + real[v, i]))
             foot = jnp.concatenate(parts, axis=0).astype(BF16)
             foot = jnp.maximum(jnp.minimum(foot, cap), jnp.zeros((), BF16))
-            got = jnp.dot(foot, wts[i], preferred_element_type=F32)
+            got = jnp.dot(foot, wts[weight_of(zz, i)], preferred_element_type=F32)
             for k in range(2):
                 res[k * SUBS + i, RES_PAD:RES_PAD + win, :] = got[k * win:(k + 1) * win]
                 if win < WIN_ROWS[0]:
@@ -220,18 +259,18 @@
 
     def messages(kind, zz, turn, half, res):
         msg = MSG_ROWS[kind]
-        reach = 2 * msg
+        spans = window_rows(kind)
         for k, v in enumerate(views(zz, turn, half)):
-            chunks = []
-            for ch in range(2):
-                total = None
-                for i in range(SUBS):
-                    term = res[k * SUBS + i, pl.ds(whole[v, ch * SUBS + i], reach), :]
-                    total = term if total is None else total + term
-                    if i % 5 == 4:
-                        yield
-                chunks.append(total)
-            part = jnp.concatenate(chunks, axis=0)
+            groups = [None] * (msg // 2)
+            for i, (first, end) in enumerate(spans):
+                term = res[k * SUBS + i, pl.ds(whole[v, i] + first, end - first), :]
+                for n in range(first // 8, end // 8):
+                    piece = term[8 * n - first:8 * n - first + 8]
+                    groups[n] = piece if groups[n] is None else groups[n] + piece
+                if i % 3 == 2:
+                    yield
+            blank = jnp.zeros((8, 128), F32)
+            part = jnp.concatenate([blank if g is None else g for g in groups], axis=0)
             high = part.astype(BF16)
             low = (part - high.astype(F32)).astype(BF16)
             h, e = real[v, SUBS + 5], real[v, SUBS + 6]
@@ -241,12 +280,11 @@
                 - jnp.maximum(centre - e * 0.5, row_low), 0.0)
             a_high = axial.astype(BF16)
             a_low = (axial - a_high.astype(F32)).astype(BF16)
-            blank = jnp.zeros((48, 128), BF16)
-            a_high = jnp.concatenate([a_high, blank], axis=0)
-            a_low = jnp.concatenate([a_low, blank], axis=0)
-            both = jnp.concatenate([a_high, a_low], axis=1)
-            rows = jnp.dot(jnp.concatenate([high, low], axis=1),
-                           jnp.concatenate([both, both], axis=0), preferred_element_type=F32)
+            a_high = jnp.concatenate([jnp.concatenate([a_high] * 4, axis=0)] * 2, axis=1)
+            a_low = jnp.concatenate([jnp.concatenate([a_low] * 4, axis=0)] * 2, axis=1)
+            rows = lax.dot_general(
+                jnp.concatenate([high, low], axis=1), jnp.concatenate([a_high, a_low], axis=0),
+                (((1,), (1,)), ((), ())), preferred_element_type=F32)
             at = 2 * half + k
             axial_rows[at, 0:4 * msg, :] = rows[:, :128] + rows[:, 128:]
             yield
@@ -269,38 +307,36 @@
         rows = SENT_ROWS[kind]
         return pltpu.make_async_remote_copy(
             sends.at[zz, turn * NY + j, pl.ds(0, rows)], lands.at[zz, block, pl.ds(0, rows)],
-            msg_send.at[zz, turn * NY + j], msg_recv.at[zz, block],
+            msg_send.at[zz], msg_recv.at[zz],
             device_id=(device(to_block(turn, j), zh, core), slab), device_id_type=MESH)
 
     def keep(kind, zz):
         rows = SENT_ROWS[kind]
         return pltpu.make_async_copy(
             sends.at[zz, 0, pl.ds(0, rows)], lands.at[zz, block, pl.ds(0, rows)],
-            msg_recv.at[zz, block])
-
-    def arrival(kind, zz, src):
-        rows = SENT_ROWS[kind]
+            msg_recv.at[zz])
+
+    def all_arrived(kind, zz):
+        rows = pl.ds(0, SENT_ROWS[kind])
+        return pltpu.make_async_copy(sends.at[zz, :, rows], lands.at[zz, :, rows], msg_recv.at[zz])
+
+    def all_sent(kind, zz):
+        rows, others = pl.ds(0, SENT_ROWS[kind]), pl.ds(1, BLOCKS - 1)
+        return pltpu.make_async_copy(
+            lands.at[zz, others, rows], sends.at[zz, others, rows], msg_send.at[zz])
+
+    def total_out(kind, turn):
+        rows = pl.ds(SPANS[kind][0], SPANS[kind][1] - SPANS[kind][0])
         return pltpu.make_async_remote_copy(
-            sends.at[zz, 0, pl.ds(0, rows)], lands.at[zz, src, pl.ds(0, rows)],
-            msg_send.at[zz, 0], msg_recv.at[zz, src],
-            device_id=(device(src, zh, core), slab), device_id_type=MESH)
-
-    def total_out(turn):
-        return pltpu.make_async_remote_copy(
-            summed.at[turn], arrived.at[turn], sum_send.at[turn], sum_recv.at[turn],
+            summed.at[turn, rows], arrived.at[turn, rows], sum_send.at[turn], sum_recv.at[turn],
             device_id=(device(block, flipped(turn), core), slab), device_id_type=MESH)
 
-    def octant(kind, zz):
+    def half_octant(kind, zz, late):
         def step(turn, carry):
             before = jnp.maximum(turn - 1, 0)
             together(footprints(kind, zz, turn, 0, res_a), messages(kind, zz, before, 1, res_b))
-
-            @pl.when(turn > 0)
-            def _():
-                message(kind, zz, turn - 1, 2).start()
-                message(kind, zz, turn - 1, 3).start()
-
             together(footprints(kind, zz, turn, 1, res_b), messages(kind, zz, turn, 0, res_a))
+            message(kind, zz, turn, 1).start()
 
             @pl.when(turn == 0)
             def _():
@@ -309,14 +345,17 @@
             @pl.when(turn > 0)
             def _():
                 message(kind, zz, turn, 0).start()
-
-            message(kind, zz, turn, 1).start()
+                message(kind, zz, turn - 1, 2).start()
+                message(kind, zz, turn - 1, 3).start()
             return carry
 
-        lax.fori_loop(0, NX, step, 0)
-        together(messages(kind, zz, NX - 1, 1, res_b))
-        message(kind, zz, NX - 1, 2).start()
-        message(kind, zz, NX - 1, 3).start()
+        lax.fori_loop(2 * late, 2 * late + 2, step, 0)
+
+        @pl.when(late == 1)
+        def _():
+            together(messages(kind, zz, NX - 1, 1, res_b))
+            message(kind, zz, NX - 1, 2).start()
+            message(kind, zz, NX - 1, 3).start()
 
     def by_kind(zz, work):
         narrow = (zz == 1) | (zz == 2)
@@ -332,20 +371,7 @@
     def gather_block(turn):
         zz = flipped(turn)
 
-        def await_all(kind):
-            def await_one(src, carry):
-                @pl.when(src == block)
-                def _():
-                    keep(kind, zz).wait()
-
-                @pl.when(src != block)
-                def _():
-                    arrival(kind, zz, src).wait_recv()
-                return carry
-
-            lax.fori_loop(0, BLOCKS, await_one, 0)
-
-        by_kind(zz, await_all)
+        by_kind(zz, lambda kind: all_arrived(kind, zz).wait())
         for src in range(BLOCKS):
             spread[src, PAD:PAD + LAND, :] = lands[zz, src]
         for ch in range(4):
@@ -355,35 +381,43 @@
                 total = term if total is None else total + term
             summed[turn, ch * PAD:(ch + 1) * PAD, :] = total
 
-    def one_octant(turn, carry):
+    def advance(n, carry):
+        turn, late = lax.div(n, 2), lax.rem(n, 2)
         zz = flipped(turn)
-        by_kind(zz, lambda kind: octant(kind, zz))
-
-        @pl.when(turn > 0)
+        by_kind(zz, lambda kind: half_octant(kind, zz, late))
+
+        @pl.when((n == 3) | (n == 5) | (n == 6))
         def _():
             gather_block(turn - 1)
-            total_out(turn - 1).start()
+            by_kind(flipped(turn - 1), lambda kind: total_out(kind, turn - 1).start())
         return carry
 
-    lax.fori_loop(0, NZH, one_octant, 0)
+    lax.fori_loop(0, 2 * NZH, advance, 0)
     gather_block(NZH - 1)
     for turn in range(NZH - 1):
-        total_out(turn).wait()
+        by_kind(flipped(turn), lambda kind, turn=turn: total_out(kind, turn).wait_send())
     out_row = lax.rem(lax.broadcasted_iota(jnp.int32, (COLS // 4, 128), 1), R_SLAB) + slab * R_SLAB
-    read_out = (out_row >= limits[tile, 0]) & (out_row < limits[tile, 1])
-    total = (arrived[0] + arrived[1]) + (arrived[2] + summed[NZH - 1])
-    out_ref[...] = jnp.where(read_out, total, 0.0)
+    read_out = (out_row >= limits[0, tile]) & (out_row < limits[1, tile])
+
+    def finish(kind):
+        first, end = SPANS[kind]
+        for turn in range(NZH - 1):
+            total_out(kind, turn).wait_recv()
+        total = (arrived[0, first:end] + arrived[1, first:end]) + (
+            arrived[2, first:end] + summed[NZH - 1, first:end])
+        if first:
+            edge = jnp.zeros((first, 128), F32)
+            total = jnp.concatenate([edge, total, edge], axis=0)
+        out_ref[...] = jnp.where(read_out, total, 0.0)
+
+    by_kind(zh, finish)
     for zz in range(NZH):
-        def drain(n, carry, zz=zz):
-            message(int(zz in (1, 2)), zz, lax.div(n, NY), lax.rem(n, NY)).wait_send()
-            return carry
-
-        lax.fori_loop(1, BLOCKS, drain, 0)
+        all_sent(int(zz in (1, 2)), zz).wait()
 
 
 def on_device(volume, fov_mask, block_angles, row_range):
     smem = pl.BlockSpec(memory_space=pltpu.SMEM)
-    anywhere = pl.BlockSpec(memory_space=pl.ANY)
+    anywhere = pl.BlockSpec(memory_space=pltpu.HBM)
     pixels = TX * TY
     packed = pl.pallas_call(
         kernel,
@@ -402,8 +436,8 @@
             pltpu.VMEM((HALO_Z, pixels), F32),
             pltpu.VMEM((HALO_Z, pixels), F32),
             pltpu.VMEM((SUBS, SUB * SUB, 128), BF16),
-            pltpu.VMEM((2 * SUBS, 2 * RES_PAD + 40, 128), F32),
-            pltpu.VMEM((2 * SUBS, 2 * RES_PAD + 40, 128), F32),
+            pltpu.VMEM((2 * SUBS, RES_ROWS, 128), F32),
+            pltpu.VMEM((2 * SUBS, RES_ROWS, 128), F32),
             pltpu.VMEM((NY, 160, 128), F32),
             pltpu.VMEM((NZH, BLOCKS, LAND, 128), F32),
             pltpu.VMEM((NZH, BLOCKS, LAND, 128), F32),
@@ -414,16 +448,16 @@
             pltpu.SemaphoreType.DMA((2,)),
             pltpu.SemaphoreType.DMA((3,)),
             pltpu.SemaphoreType.DMA((3,)),
-            pltpu.SemaphoreType.DMA((NZH, BLOCKS)),
-            pltpu.SemaphoreType.DMA((NZH, BLOCKS)),
+            pltpu.SemaphoreType.DMA((NZH,)),
+            pltpu.SemaphoreType.DMA((NZH,)),
             pltpu.SemaphoreType.DMA((NZH - 1,)),
             pltpu.SemaphoreType.DMA((NZH - 1,)),
         ],
         compiler_params=pltpu.CompilerParams(
-            collective_id=0, has_side_effects=True, vmem_limit_bytes=44 * 1024 * 1024),
+            collective_id=0, has_side_effects=True, vmem_limit_bytes=54912 * 1024),
         cost_estimate=pl.CostEstimate(
             flops=64 * 16 * 40 * 256 * 128 * 2, bytes_accessed=1 << 20, transcendentals=0),
-    )(block_angles, row_range, volume, fov_mask)
+    )(block_angles, row_range.T, volume, fov_mask)
     return packed.reshape(COLS // 4, 4, R_SLAB).transpose(2, 0, 1).reshape(1, R_SLAB, COLS)
 
 

time: 51.9 us -> 42.2 us (0.81)
  the two profiles are of different devices: /device:TPU:33 before, /device:TPU:1 now
where the time goes in v4:
time: 42.2 us; the launch traced here: 41.5 us
  Pallas kernels  39 us (92%)
  local copies, waits for them, and re-layouts  2.53 us (6%)
    pallas_call x1, Pallas kernels, on_device(): pl.pallas_call(kernel, out_shape=jax.ShapeDtypeStruct((COLS // 4, 128), F...  39 us
    unnamed x6, local copies, waits for them, and re-layouts  1.38 us

profile of v4, /device:TPU:1, one launch (start us, length us, event | category | flops | bytes accessed | tf_op | source)
XLA Modules:
  0.0 41.5 jit_solution(16263638328817565720)
XLA Ops:
  0.0 0.0 copy-start.1
  0.0 0.0 copy-start.2
  0.0 0.7 %copy-done.1 = s32[128,2]{0,1:T(2,128)S(1)} copy-done((s32[128,2]{0,1:T(2,128)S(1)}, s32[128,2]{0,1:T(2,128)}, u32[]{:S(2)}) %copy-start.1) | copy-done | bytes 1048
  0.7 0.0 copy-done.2
  0.7 0.0 copy-start
  0.7 0.7 %copy-done = s32[1,2048]{1,0:T(1,128)S(1)} copy-done((s32[1,2048]{1,0:T(1,128)S(1)}, s32[1,2048]{1,0:T(1,128)}, u32[]{:S(2)}) %copy-start) | copy-done | bytes 8216
  1.4 39.0 %shard_map.46 = f32[256,128]{1,0:T(8,128)S(1)} custom-call(s32[16]{0:T(128)S(1)} %copy-done.2, s32[2,128]{1,0:T(2,128)S(1)} %bitcast.5, bf16[1,64,2048]{2,1,0:T(8,128)(2,1)} %vol_hbm.1, s32[1,2048]{1,0:T(1,128)S(1)} %copy-done), custom_call_target="tpu_custom_call" | custom-call | flops 2684354560 | bytes 1048576 | tf_op jit(solution)/shard_map/pallas_call | solution.py:422
  40.4 0.1 copy.6
  40.5 0.2 copy.7
  40.7 0.8 %copy.8 = f32[1,32,1024]{2,1,0:T(8,128)} copy(f32[1,32,1024]{1,2,0:T(8,128)S(1)} %bitcast.6) | data formatting | bytes 262144 | tf_op jit(solution)/shard_map/reshape | solution.py:461
Async XLA Ops:
  0.0 0.7 %copy-start.1 = (s32[128,2]{0,1:T(2,128)S(1)}, s32[128,2]{0,1:T(2,128)}, u32[]{:S(2)}) copy-start(s32[128,2]{0,1:T(2,128)} %param.7) | copy-start | bytes 3076
  0.0 0.7 %copy-start.2 = (s32[16]{0:T(128)S(1)}, s32[16]{0:T(128)}, u32[]{:S(2)}) copy-start(s32[16]{0:T(128)} %angles.1) | copy-start | bytes 196
  0.7 0.7 %copy-start = (s32[1,2048]{1,0:T(1,128)S(1)}, s32[1,2048]{1,0:T(1,128)}, u32[]{:S(2)}) copy-start(s32[1,2048]{1,0:T(1,128)} %mask_hbm.1) | copy-start | bytes 24580

commit v5 on v4

--- a/solution.py
+++ b/solution.py
@@ -438,7 +438,7 @@
             pltpu.VMEM((SUBS, SUB * SUB, 128), BF16),
             pltpu.VMEM((2 * SUBS, RES_ROWS, 128), F32),
             pltpu.VMEM((2 * SUBS, RES_ROWS, 128), F32),
-            pltpu.VMEM((NY, 160, 128), F32),
+            pltpu.VMEM((NY, 168, 128), F32),
             pltpu.VMEM((NZH, BLOCKS, LAND, 128), F32),
             pltpu.VMEM((NZH, BLOCKS, LAND, 128), F32),
             pltpu.VMEM((BLOCKS, LAND + 2 * PAD, 128), F32),

time: 42.2 us -> 42.2 us (level)
  no operation moved by 1% of the time
where the time goes in v5:
time: 42.2 us; the launch traced here: 41.5 us
  Pallas kernels  38.9 us (92%)
  local copies, waits for them, and re-layouts  2.53 us (6%)
    pallas_call x1, Pallas kernels, on_device(): pl.pallas_call(kernel, out_shape=jax.ShapeDtypeStruct((COLS // 4, 128), F...  38.9 us
    unnamed x6, local copies, waits for them, and re-layouts  1.38 us

profile of v5, /device:TPU:1, one launch (start us, length us, event | category | flops | bytes accessed | tf_op | source)
XLA Modules:
  0.0 41.5 jit_solution(11395616001899920797)
XLA Ops:
  0.0 0.0 copy-start.1
  0.0 0.0 copy-start.2
  0.0 0.7 %copy-done.1 = s32[128,2]{0,1:T(2,128)S(1)} copy-done((s32[128,2]{0,1:T(2,128)S(1)}, s32[128,2]{0,1:T(2,128)}, u32[]{:S(2)}) %copy-start.1) | copy-done | bytes 1048
  0.7 0.0 copy-done.2
  0.7 0.0 copy-start
  0.7 0.7 %copy-done = s32[1,2048]{1,0:T(1,128)S(1)} copy-done((s32[1,2048]{1,0:T(1,128)S(1)}, s32[1,2048]{1,0:T(1,128)}, u32[]{:S(2)}) %copy-start) | copy-done | bytes 8216
  1.4 38.9 %shard_map.46 = f32[256,128]{1,0:T(8,128)S(1)} custom-call(s32[16]{0:T(128)S(1)} %copy-done.2, s32[2,128]{1,0:T(2,128)S(1)} %bitcast.5, bf16[1,64,2048]{2,1,0:T(8,128)(2,1)} %vol_hbm.1, s32[1,2048]{1,0:T(1,128)S(1)} %copy-done), custom_call_target="tpu_custom_call" | custom-call | flops 2684354560 | bytes 1048576 | tf_op jit(solution)/shard_map/pallas_call | solution.py:422
  40.3 0.1 copy.6
  40.4 0.2 copy.7
  40.6 0.8 %copy.8 = f32[1,32,1024]{2,1,0:T(8,128)} copy(f32[1,32,1024]{1,2,0:T(8,128)S(1)} %bitcast.6) | data formatting | bytes 262144 | tf_op jit(solution)/shard_map/reshape | solution.py:461
Async XLA Ops:
  0.0 0.7 %copy-start.1 = (s32[128,2]{0,1:T(2,128)S(1)}, s32[128,2]{0,1:T(2,128)}, u32[]{:S(2)}) copy-start(s32[128,2]{0,1:T(2,128)} %param.7) | copy-start | bytes 3076
  0.0 0.7 %copy-start.2 = (s32[16]{0:T(128)S(1)}, s32[16]{0:T(128)}, u32[]{:S(2)}) copy-start(s32[16]{0:T(128)} %angles.1) | copy-start | bytes 196
  0.7 0.7 %copy-start = (s32[1,2048]{1,0:T(1,128)S(1)}, s32[1,2048]{1,0:T(1,128)}, u32[]{:S(2)}) copy-start(s32[1,2048]{1,0:T(1,128)} %mask_hbm.1) | copy-start | bytes 24580
